TPU v7x, 512 devices: a whole 4x8x8 slice. The times are simulated.
512 devices in a mesh: tm: 64 (over x, z, core), rows: 8 (over y).
Axes of the slice: x: 4, y: 8, z: 8, core: 2. Of those that a mesh axis runs over, the one named last changes fastest.
Arguments:
- returns: float32 [4096, 16384], P('tm', 'rows'), may hold values from -6 to 6
- variances: float32 [4096, 16384], P('tm', 'rows'), may hold values from 0.3 to 6
- loadings: float32 [16384], P('rows'), may hold values from -4 to 4
- sector: int32 [16384], P('rows'), may hold values from 0 to 511
- persistence: float32 [512], replicated, may hold values from 0.9 to 1, as said below
- factor_noise: float32 [4096, 512], P('tm'), may hold values from 0 to 200, as said below
Outputs:
- smoothed_mean: float32 [4096, 512], P('tm', 'rows')
- log_variance: float32 [4096, 512], P('tm', 'rows')
Inputs may be any that keep to these rules, and one draw needn't show every extreme that they name: `persistence`: each coefficient lies strictly between 0 and 1. `factor_noise`: every entry is positive.
All inputs are finite; a program needn't handle non-finite values.
Results may differ from a plain program's by a relative error of at most 0.00065.
Values sent between devices are 32-bit elements; how exact they have to be, the bound alone decides.
No kernel may reach another device: no remote copies, remote signals or barrier semaphores. Data moves between devices by JAX's collectives and lax.ppermute only.
A program may use at most 64 MiB of HBM per device.

v0:
```python
import math

import jax
import jax.numpy as jnp
from jax import lax
from jax.sharding import PartitionSpec as P


def carried_in(value, axis, join, neutral, backward):
    count, mine = (lax.axis_size(axis), lax.axis_index(axis))
    pieces = jax.tree.map(lambda part: lax.all_gather(part, axis), value)
    if backward:
        pieces = jax.tree.map(lambda part: part[::-1], pieces)
        mine = count - 1 - mine
    so_far = jax.tree.map(
        lambda part, zero: jnp.full_like(part, 0) + jnp.asarray(zero, part.dtype), value, neutral
    )

    def hop(position, so_far):
        longer = join(so_far, jax.tree.map(lambda part: part[position], pieces))
        return jax.tree.map(lambda new, old: jnp.where(position < mine, new, old), longer, so_far)

    return lax.fori_loop(0, count - 1, hop, so_far)


def passed_along(x, axis, by):
    size = lax.axis_size(axis)
    pairs = [(i, i + by) for i in range(size) if 0 <= i + by < size]
    return lax.ppermute(x, axis, pairs)


def combine_filter(earlier, later):
    left_gain, left_mean, left_cov, left_info, left_prec = earlier
    right_gain, right_mean, right_cov, right_info, right_prec = later
    inverse = 1.0 / (1.0 + left_cov * right_prec)
    return (
        right_gain * left_gain * inverse,
        right_gain * (left_mean + left_cov * right_info) * inverse + right_mean,
        right_gain * right_gain * left_cov * inverse + right_cov,
        left_gain * (right_info - right_prec * left_mean) * inverse + left_info,
        left_gain * left_gain * right_prec * inverse + left_prec,
    )


def combine_smooth(earlier, later):
    high_gain, high_mean, high_square, high_var = earlier
    low_gain, low_mean, lower_square_term, low_var = later
    return (
        low_gain * high_gain,
        low_gain * high_mean + low_mean,
        lower_square_term * high_square,
        lower_square_term * high_var + low_var,
    )


def filter_identity(local_width):
    ones = jnp.ones((local_width,), jnp.float32)
    zeros = jnp.zeros((local_width,), jnp.float32)
    return (ones, zeros, zeros, zeros, zeros)


def smooth_identity(local_width):
    ones = jnp.ones((local_width,), jnp.float32)
    zeros = jnp.zeros((local_width,), jnp.float32)
    return (ones, zeros, ones, zeros)


def body(returns, variances, loadings, sector, persistence, factor_noise):
    bars_dev, series_dev = returns.shape
    factors = persistence.shape[0]
    weights = 1.0 / variances
    stacked = jnp.concatenate(
        [returns * weights * loadings[None, :], weights * (loadings * loadings)[None, :]], axis=0
    )
    block_size = math.gcd(series_dev, 512)
    block_count = series_dev // block_size
    column_total = lax.broadcasted_iota(jnp.int32, (block_size, factors), 1)

    def add_block(block_index, running):
        block_start = block_index * block_size
        block_cols = lax.dynamic_slice_in_dim(stacked, block_start, block_size, 1)
        owners = lax.dynamic_slice_in_dim(sector, block_start, block_size, 0)
        one_hot = (owners[:, None] == column_total).astype(jnp.float32)
        return running + jnp.dot(
            block_cols, one_hot, precision=lax.Precision.HIGHEST, preferred_element_type=jnp.float32
        )

    projected = lax.fori_loop(
        0, block_count, add_block, jnp.zeros((2 * bars_dev, factors), jnp.float32)
    )
    signal = projected[:bars_dev]
    information = projected[bars_dev:]
    share = factors // lax.axis_size("rows")
    offset = lax.axis_index("rows") * share
    signal, information = lax.psum((signal, information), "rows")
    local_width = signal.shape[1]
    decay_row = persistence[None, :]
    position = lax.axis_index("tm")
    devices = lax.axis_size("tm")
    inverse = 1.0 / (1.0 + factor_noise * information)
    elements = (
        decay_row * inverse,
        factor_noise * signal * inverse,
        factor_noise * inverse,
        decay_row * signal * inverse,
        decay_row * decay_row * information * inverse,
    )
    prefix = lax.associative_scan(combine_filter, elements)
    combined_kalman_weight, sum_mean, sum_cov, sum_info, sum_prec = (
        prefix[0][-1],
        prefix[1][-1],
        prefix[2][-1],
        prefix[3][-1],
        prefix[4][-1],
    )
    incoming = carried_in(
        (combined_kalman_weight, sum_mean, sum_cov, sum_info, sum_prec),
        "tm",
        combine_filter,
        filter_identity(local_width),
        False,
    )
    filtered = combine_filter(tuple((member[None, :] for member in incoming)), prefix)
    filt_mean = filtered[1]
    filt_cov = filtered[2]
    noise_ahead = passed_along(factor_noise[:1], "tm", -1)
    noise_next = jnp.concatenate([factor_noise[1:], noise_ahead], axis=0)
    ahead = decay_row * decay_row * filt_cov + noise_next
    bar_index = lax.broadcasted_iota(jnp.int32, filt_cov.shape, 0)
    final_bar = (position == devices - 1) & (bar_index == bars_dev - 1)
    smooth_gain = jnp.where(final_bar, 0.0, decay_row * filt_cov / ahead)
    remain = jnp.where(final_bar, 1.0, noise_next / ahead)
    backward = (smooth_gain, remain * filt_mean, smooth_gain * smooth_gain, remain * filt_cov)
    flipped = lax.associative_scan(combine_smooth, tuple((member[::-1] for member in backward)))
    suffix = tuple((member[::-1] for member in flipped))
    head_gain, head_mean, head_square, head_var = (
        suffix[0][0],
        suffix[1][0],
        suffix[2][0],
        suffix[3][0],
    )
    incoming_back = carried_in(
        (head_gain, head_mean, head_square, head_var),
        "tm",
        combine_smooth,
        smooth_identity(local_width),
        True,
    )
    smoothed_mean = suffix[0] * incoming_back[1][None, :] + suffix[1]
    smoothed_var = suffix[2] * incoming_back[3][None, :] + suffix[3]
    log_variance = jnp.log(smoothed_var)
    return (
        lax.dynamic_slice_in_dim(smoothed_mean, offset, share, 1),
        lax.dynamic_slice_in_dim(log_variance, offset, share, 1),
    )


def solution(mesh):
    in_specs = (P("tm", "rows"), P("tm", "rows"), P("rows"), P("rows"), P(), P("tm", None))
    out_specs = (P("tm", "rows"), P("tm", "rows"))
    return jax.shard_map(body, mesh=mesh, in_specs=in_specs, out_specs=out_specs, check_vma=False)
```

profile of v0, /device:TPU:1, one launch (start us, length us, event | category | flops | bytes accessed | tf_op | source)
XLA Modules:
  0.0 569.3 jit_solution(17268241305834412332)
XLA Ops:
  7.2 0.8 mul.840
  8.0 1.3 multiply_multiply_fusion
  9.4 5.5 while.46
  9.5 0.8 dynamic_slice.131
  10.2 0.6 convolution_add_fusion.2
  10.8 0.8 dynamic_slice.131
  11.6 0.6 convolution_add_fusion.2
  12.2 0.8 dynamic_slice.131
  13.0 0.6 convolution_add_fusion.2
  13.6 0.8 dynamic_slice.131
  14.4 0.6 convolution_add_fusion.2
  15.0 0.7 fusion.32
  15.8 0.9 copy-done
  16.6 8.8 %collective-permute-start = (f32[1,512]{1,0:T(1,128)S(1)}, f32[1,512]{1,0:T(1,128)S(1)}, u32[]{:S(2)}, u32[]{:S(2)}) collective-permute-start(f32[1,512]{1,0:T(1,128)S(1)} %slice.991), channel_id=1, source_target_pairs={{8,0},{16,8},{24,16},{32,24},{40,32},{48,40},{56,48},{64,56},{72,6... | collective-permute-start | bytes 6152 | tf_op jit(solution)/shard_map/ppermute | solution.py:29
  25.5 0.7 copy-done.2
  26.2 68.0 %all-reduce.111.cloned.1.call-done = (f32[64,512]{1,0:T(8,128)}, f32[64,512]{1,0:T(8,128)}) async-done(((f32[64,512]{1,0:T(8,128)}, f32[64,512]{1,0:T(8,128)}), (f32[64,512]{1,0:T(8,128)}, f32[64,512]{1,0:T(8,128)})) %all-reduce.111.cloned.1.call-update) | async-done | bytes 262160 | tf_op jit(solution)/shard_map/psum | solution.py:95
  94.2 1.0 multiply_multiply_fusion.2
  98.8 56.5 %all-gather.4 = f32[64,1,512]{2,1,0:T(1,128)S(1)} all-gather(f32[1,1,512]{2,1,0:T(1,128)S(1)} %add_bitcast_fusion.4), channel_id=1, replica_groups=mesh['tm'=64,'rows'=8] {'tm'}, dimensions={0}, use_global_device_ids=true | all-gather | bytes 133120 | tf_op jit(solution)/shard_map/all_gather | solution.py:11
  156.0 48.3 %all-gather.3 = f32[64,1,512]{2,1,0:T(1,128)S(1)} all-gather(f32[1,1,512]{2,1,0:T(1,128)S(1)} %add_bitcast_fusion.5), channel_id=1, replica_groups=mesh['tm'=64,'rows'=8] {'tm'}, dimensions={0}, use_global_device_ids=true | all-gather | bytes 133120 | tf_op jit(solution)/shard_map/all_gather | solution.py:11
  204.5 47.6 %all-gather.2 = f32[64,1,512]{2,1,0:T(1,128)S(1)} all-gather(f32[1,1,512]{2,1,0:T(1,128)S(1)} %add_bitcast_fusion.6), channel_id=1, replica_groups=mesh['tm'=64,'rows'=8] {'tm'}, dimensions={0}, use_global_device_ids=true | all-gather | bytes 133120 | tf_op jit(solution)/shard_map/all_gather | solution.py:11
  252.2 48.3 %all-gather.1 = f32[64,1,512]{2,1,0:T(1,128)S(1)} all-gather(f32[1,1,512]{2,1,0:T(1,128)S(1)} %add_bitcast_fusion.7), channel_id=1, replica_groups=mesh['tm'=64,'rows'=8] {'tm'}, dimensions={0}, use_global_device_ids=true | all-gather | bytes 133120 | tf_op jit(solution)/shard_map/all_gather | solution.py:11
  300.6 47.6 %all-gather = f32[64,1,512]{2,1,0:T(1,128)S(1)} all-gather(f32[1,1,512]{2,1,0:T(1,128)S(1)} %add_bitcast_fusion.8), channel_id=1, replica_groups=mesh['tm'=64,'rows'=8] {'tm'}, dimensions={0}, use_global_device_ids=true | all-gather | bytes 133120 | tf_op jit(solution)/shard_map/all_gather | solution.py:11
  348.3 6.6 %while.47 = (s32[]{:T(128)}, f32[512]{0:T(512)S(1)}, f32[512]{0:T(512)S(1)}, s32[]{:T(128)}, f32[64,512]{1,0:T(8,128)S(1)}, /*index=5*/f32[64,512]{1,0:T(8,128)S...) while((s32[]{:T(128)}, f32[512]{0:T(512)S(1)}, ...), condition=%wide.region_5.6_spmd.clone, body=%wide.region_4.5_spmd.clone.sunk | while | flops 8196 | bytes 39053 | solution.py:23
  355.0 0.2 fusion.31
  357.2 0.1 slice.1114
  360.4 48.5 %all-gather.8 = f32[64,1,512]{2,1,0:T(1,128)S(1)} all-gather(f32[1,1,512]{2,1,0:T(1,128)S(1)} %add_bitcast_fusion), channel_id=1, replica_groups=mesh['tm'=64,'rows'=8] {'tm'}, dimensions={0}, use_global_device_ids=true | all-gather | bytes 133120 | tf_op jit(solution)/shard_map/all_gather | solution.py:11
  409.1 47.6 %all-gather.7 = f32[64,1,512]{2,1,0:T(1,128)S(1)} all-gather(f32[1,1,512]{2,1,0:T(1,128)S(1)} %add_bitcast_fusion.1), channel_id=1, replica_groups=mesh['tm'=64,'rows'=8] {'tm'}, dimensions={0}, use_global_device_ids=true | all-gather | bytes 133120 | tf_op jit(solution)/shard_map/all_gather | solution.py:11
  456.8 48.3 %all-gather.6 = f32[64,1,512]{2,1,0:T(1,128)S(1)} all-gather(f32[1,1,512]{2,1,0:T(1,128)S(1)} %add_bitcast_fusion.2), channel_id=1, replica_groups=mesh['tm'=64,'rows'=8] {'tm'}, dimensions={0}, use_global_device_ids=true | all-gather | bytes 133120 | tf_op jit(solution)/shard_map/all_gather | solution.py:11
  505.3 47.6 %all-gather.5 = f32[64,1,512]{2,1,0:T(1,128)S(1)} all-gather(f32[1,1,512]{2,1,0:T(1,128)S(1)} %add_bitcast_fusion.3), channel_id=1, replica_groups=mesh['tm'=64,'rows'=8] {'tm'}, dimensions={0}, use_global_device_ids=true | all-gather | bytes 133120 | tf_op jit(solution)/shard_map/all_gather | solution.py:11
  553.1 7.6 %while.48 = (s32[]{:T(128)}, f32[512]{0:T(512)S(1)}, f32[512]{0:T(512)S(1)}, s32[]{:T(128)}, f32[64,512]{1,0:T(8,128)S(1)}, /*index=5*/f32[64,512]{1,0:T(8,128)S...) while((s32[]{:T(128)}, f32[512]{0:T(512)S(1)}, f32[512]{0:T(512)S(1)}, ...), condition=%wide.region_7.8_spmd.clone, body=%wide.region_6.7_spmd.clone.sunk | while | flops 4100 | bytes 32905 | solution.py:23
  561.1 0.7 fusion.8
  561.8 0.7 dynamic-slice_add_fusion.1
  (1014 shorter events, 16.2 us)
Async XLA Ops:
  7.2 87.0 %all-reduce.111.cloned.1.call-start = ((), (), s32[]{:S(2)}) async-start(), calls=%async_computation | async-start | bytes 524288 | tf_op jit(solution)/shard_map/psum | solution.py:95
  7.2 0.8 copy-start.1
  15.7 0.9 copy-start
  16.6 338.2 %collective-permute-start = (f32[1,512]{1,0:T(1,128)S(1)}, f32[1,512]{1,0:T(1,128)S(1)}, u32[]{:S(2)}, u32[]{:S(2)}) collective-permute-start(f32[1,512]{1,0:T(1,128)S(1)} %slice.991), channel_id=1, source_target_pairs={{8,0},{16,8},{24,16},{32,24},{40,32},{48,40},{56,48},{64,56},{72,6... | collective-permute-start | bytes 6152 | tf_op jit(solution)/shard_map/ppermute | solution.py:29
  25.5 0.7 copy-start.2
Sparse Core Ops, SparseCore 0:
  15.9 78.2 all-reduce.110
where the time goes:
time: 570 us; the launch traced here: 569 us
  blocking collectives  441 us (77%)
  waiting for transfers between devices  68 us (12%)
  local copies, waits for them, and re-layouts  17.4 us (3%)
  between operations  16.4 us (3%)
  other arithmetic  8.97 us (2%)
  starting transfers between devices  8.81 us (2%)
  loops' own time  6.71 us (1%)
    all_gather x9, blocking collectives, carried_in(): pieces = jax.tree.map(lambda part: lax.all_gather(part, axis), value)  441 us
    psum x1, waiting for transfers between devices, body(): signal, information = lax.psum((signal, information), 'rows')  68 us
  transfers between devices with their start and end apart: 2, of which 1 were waited for; matrix products, arithmetic and copies ran while one was open for 1% of the time, Pallas kernels for 0%

commit v1 on v0

v1 whole, which is shorter than its diff:
```python
import functools

import jax
import jax.numpy as jnp
from jax import lax
from jax.experimental import pallas as pl
from jax.experimental.pallas import tpu as pltpu
from jax.sharding import PartitionSpec as P

SUB = 8
LANES = 128
HALF = 64


def combine(earlier, later):
    left_gain, left_mean, left_cov, left_info, left_prec = earlier
    right_gain, right_mean, right_cov, right_info, right_prec = later
    inverse = 1.0 / (1.0 + left_cov * right_prec)
    right_scaled = right_gain * inverse
    left_scaled = left_gain * inverse
    return (
        right_scaled * left_gain,
        right_scaled * (left_mean + left_cov * right_info) + right_mean,
        right_scaled * right_gain * left_cov + right_cov,
        left_scaled * (right_info - right_prec * left_mean) + left_info,
        left_scaled * left_gain * right_prec + left_prec,
    )


def keep(mask, element):
    return tuple(jnp.where(mask, part, fill) for part, fill in zip(element, (1.0, 0.0, 0.0, 0.0, 0.0)))


def rolled(element, shift, axis):
    return tuple(pltpu.roll(part, shift, axis) for part in element)


def iotas():
    lane = lax.broadcasted_iota(jnp.int32, (SUB, LANES), 1)
    sub = lax.broadcasted_iota(jnp.int32, (SUB, LANES), 0)
    return lane, sub


def project_kernel(returns_ref, variances_ref, loadings_ref, sector_ref, out_ref):
    bars, series = returns_ref.shape
    peers = out_ref.shape[0]
    factors = peers * HALF
    loadings = loadings_ref[...]
    scaled = loadings / variances_ref[...]
    stacked = jnp.concatenate([returns_ref[...] * scaled, scaled * loadings], axis=0)
    upper = stacked.astype(jnp.bfloat16)
    lower = (stacked - upper.astype(jnp.float32)).astype(jnp.bfloat16)
    owner = lax.broadcasted_iota(jnp.int32, (factors, series), 0)
    one_hot = jnp.where(owner == sector_ref[...], 1.0, 0.0).astype(jnp.bfloat16)
    both = lax.dot_general(
        jnp.concatenate([upper, lower], axis=0),
        one_hot,
        (((1,), (1,)), ((), ())),
        preferred_element_type=jnp.float32,
    )
    total = both[: 2 * bars] + both[2 * bars :]
    half = bars // 2
    low_lanes = lax.broadcasted_iota(jnp.int32, (half, LANES), 1) < HALF
    for pair in range(factors // LANES):
        columns = slice(pair * LANES, (pair + 1) * LANES)
        for kind in range(2):
            first = total[kind * bars : kind * bars + half, columns]
            second = total[kind * bars + half : (kind + 1) * bars, columns]
            rows = slice(kind * half, (kind + 1) * half)
            out_ref[2 * pair, rows, :] = jnp.where(low_lanes, first, pltpu.roll(second, HALF, 1))
            out_ref[2 * pair + 1, rows, :] = jnp.where(low_lanes, pltpu.roll(first, HALF, 1), second)


def block_kernel(parts_ref, noise_ref, decay_ref, local_ref, summary_ref):
    peers, rows, _ = parts_ref.shape
    half = rows // 2
    depth = half // SUB
    lane, sub = iotas()
    decay = decay_ref[...]
    elements = []
    for step in range(depth):
        signal = parts_ref[0, pl.ds(step, SUB, stride=depth), :]
        information = parts_ref[0, pl.ds(half + step, SUB, stride=depth), :]
        for peer in range(1, peers):
            signal += parts_ref[peer, pl.ds(step, SUB, stride=depth), :]
            information += parts_ref[peer, pl.ds(half + step, SUB, stride=depth), :]
        noise = noise_ref[pl.ds(step, SUB, stride=depth), :]
        inverse = 1.0 / (1.0 + noise * information)
        decayed = decay * inverse
        scaled = noise * inverse
        elements.append((decayed, scaled * signal, scaled, decayed * signal, decay * decayed * information))
    forward = [elements[0]]
    for step in range(1, depth):
        forward.append(combine(forward[-1], elements[step]))
    backward = [None] * depth
    running = elements[-1]
    for step in range(depth - 2, -1, -1):
        backward[step] = running
        running = combine(elements[step], running)
    total = forward[-1]
    ahead, behind = total, total
    for shift in (1, 2, 4):
        ahead = combine(keep(sub >= shift, rolled(ahead, shift, 0)), ahead)
        behind = combine(behind, keep(sub < SUB - shift, rolled(behind, SUB - shift, 0)))
    other = tuple(
        jnp.broadcast_to(pltpu.roll(part[SUB - 1 :, :], HALF, 1), (SUB, LANES)) for part in ahead
    )
    before = combine(keep(lane >= HALF, other), keep(sub >= 1, rolled(ahead, 1, 0)))
    after = combine(keep(sub < SUB - 1, rolled(behind, SUB - 1, 0)), keep(lane < HALF, other))
    whole = combine(other, ahead)
    turned = rolled(whole, HALF, 1)
    rows_out = (
        jnp.where(lane < HALF, turned[0], whole[1]),
        jnp.where(lane < HALF, turned[2], whole[3]),
        jnp.where(lane < HALF, turned[4], whole[4]),
    )
    for row in range(3):
        summary_ref[row : row + 1, :] = rows_out[row][SUB - 1 :, :]
    summary_ref[3:4, :] = rows_out[2][SUB - 1 :, :]
    slot = 0
    for element in (before, after, *forward, *backward[:-1]):
        for part in element:
            local_ref[slot] = part
            slot += 1


def finish_kernel(place_ref, local_ref, gathered_ref, mean_ref, log_ref):
    blocks = gathered_ref.shape[0] // 4
    depth = (local_ref.shape[0] // 5 - 1) // 2
    strip = blocks // SUB
    mine = place_ref[0]
    lane, sub = iotas()
    low = lane < HALF
    pieces = []
    for step in range(strip):
        raw = [gathered_ref[pl.ds(4 * step + kind, SUB, stride=4 * strip), :] for kind in range(3)]
        turn = [pltpu.roll(part, HALF, 1) for part in raw[:2]]
        element = (
            jnp.where(low, raw[0], turn[0]),
            jnp.where(low, turn[0], raw[0]),
            jnp.where(low, raw[1], turn[1]),
            jnp.where(low, turn[1], raw[1]),
            raw[2],
        )
        block = sub * strip + step
        pieces.append(keep(jnp.where(low, block - mine, mine - block) < 0, element))
    while len(pieces) > 1:
        pieces = [combine(pieces[i], pieces[i + 1]) for i in range(0, len(pieces), 2)]
    total = pieces[0]
    for shift in (1, 2, 4):
        total = combine(total, rolled(total, SUB - shift, 0))
    own = [part[:1, :] for part in total]
    turn = [pltpu.roll(part, HALF, 1) for part in own]
    low_row = low[:1, :]
    mean_in = jnp.where(low_row, own[1], turn[1])
    cov_in = jnp.where(low_row, own[2], turn[2])
    info_in = jnp.where(low_row, turn[3], own[3])
    prec_in = jnp.where(low_row, turn[4], own[4])

    def element_at(index):
        return tuple(local_ref[5 * index + part] for part in range(5))

    def push(mean, cov, element):
        gain, shift_mean, shift_cov, info, prec = element
        scaled = gain / (1.0 + cov * prec)
        return scaled * (mean + cov * info) + shift_mean, scaled * gain * cov + shift_cov

    def pull(info, prec, element):
        gain, shift_mean, shift_cov, own_info, own_prec = element
        scaled = gain / (1.0 + shift_cov * prec)
        return scaled * (info - prec * shift_mean) + own_info, scaled * gain * prec + own_prec

    mean_in, cov_in = push(mean_in, cov_in, element_at(0))
    info_in, prec_in = pull(info_in, prec_in, element_at(1))
    for step in range(depth):
        mean, cov = push(mean_in, cov_in, element_at(2 + step))
        if step < depth - 1:
            info, prec = pull(info_in, prec_in, element_at(2 + depth + step))
        else:
            info, prec = info_in, prec_in
        inverse = 1.0 / (1.0 + cov * prec)
        smoothed = (mean + cov * info) * inverse
        logged = jnp.log(cov * inverse)
        for ref, value in ((mean_ref, smoothed), (log_ref, logged)):
            ref[pl.ds(step, SUB, stride=depth), :] = value[:, :HALF]
            ref[pl.ds(SUB * depth + step, SUB, stride=depth), :] = pltpu.roll(value, HALF, 1)[:, :HALF]


VMEM = pl.BlockSpec(memory_space=pltpu.VMEM)
SMEM = pl.BlockSpec(memory_space=pltpu.SMEM)


def body(returns, variances, loadings, sector, persistence, factor_noise):
    bars, series = returns.shape
    peers = lax.axis_size("rows")
    blocks = lax.axis_size("tm")
    half = bars // 2
    depth = half // SUB
    count = 2 * depth + 1
    sends = pl.pallas_call(
        project_kernel,
        out_shape=jax.ShapeDtypeStruct((peers, bars, LANES), jnp.float32),
        in_specs=[VMEM] * 4,
        out_specs=VMEM,
        compiler_params=pltpu.CompilerParams(vmem_limit_bytes=32 * 1024 * 1024),
    )(returns, variances, loadings[None, :], sector[None, :])
    offset = lax.axis_index("rows") * HALF
    noise = lax.dynamic_slice_in_dim(factor_noise, offset, HALF, 1)
    noise = jnp.concatenate([noise[:half], noise[half:]], axis=1)
    decay = lax.dynamic_slice_in_dim(persistence, offset, HALF, 0)
    decay = jnp.concatenate([decay, decay])[None, :]
    parts = lax.all_to_all(sends, "rows", 0, 0)
    local, summary = pl.pallas_call(
        block_kernel,
        out_shape=(
            jax.ShapeDtypeStruct((5 * count, SUB, LANES), jnp.float32),
            jax.ShapeDtypeStruct((4, LANES), jnp.float32),
        ),
        in_specs=[VMEM] * 3,
        out_specs=(VMEM, VMEM),
    )(parts, noise, decay)
    spread = jnp.broadcast_to(summary[None], (blocks, 4, LANES))
    gathered = lax.all_to_all(spread, "tm", 0, 0)
    place = jnp.reshape(lax.axis_index("tm"), (1,)).astype(jnp.int32)
    return pl.pallas_call(
        finish_kernel,
        out_shape=(
            jax.ShapeDtypeStruct((bars, HALF), jnp.float32),
            jax.ShapeDtypeStruct((bars, HALF), jnp.float32),
        ),
        in_specs=[SMEM, VMEM, VMEM],
        out_specs=(VMEM, VMEM),
    )(place, local, gathered.reshape(blocks * 4, LANES))


def solution(mesh):
    in_specs = (P("tm", "rows"), P("tm", "rows"), P("rows"), P("rows"), P(), P("tm", None))
    out_specs = (P("tm", "rows"), P("tm", "rows"))
    return jax.shard_map(body, mesh=mesh, in_specs=in_specs, out_specs=out_specs, check_vma=False)
```

time: 570 us -> 56.9 us (0.10)
  blocking collectives: 441 us -> 0 us
  waiting for transfers between devices: 68 us -> 16.9 us
  between operations: 16.4 us -> 0.66 us
  starting transfers between devices: 8.81 us -> 24.4 us
  local copies, waits for them, and re-layouts: 17.4 us -> 7.71 us
  other arithmetic: 8.97 us -> 1.28 us
  loops' own time: 6.71 us -> 0 us
    all_gather x9 -> x0, blocking collectives: 441 us -> none  [carried_in(): pieces = jax.tree.map(lambda part: lax.all_gather(part, axis), value)]
    psum x1 -> x0, waiting for transfers between devices: 68 us -> none  [body(): signal, information = lax.psum((signal, information), 'rows')]
    all_to_all x0 -> x2, starting transfers between devices: none -> 24.4 us  [the longest x1 16.8 us: body(): gathered = lax.all_to_all(spread, 'tm', 0, 0)]
    all_to_all x0 -> x2, waiting for transfers between devices: none -> 16.9 us  [the longest x1 10.4 us: body(): gathered = lax.all_to_all(spread, 'tm', 0, 0)]
    ppermute x1 -> x0, starting transfers between devices: 8.78 us -> none  [passed_along(): return lax.ppermute(x, axis, pairs)]
    dynamic_slice x447 -> x1, local copies, waits for them, and re-layouts: 8.65 us -> 0.75 us  [body(): decay = lax.dynamic_slice_in_dim(persistence, offset, HALF, 0)]
    another operation x3 -> x0, loops' own time: 6.71 us -> none  [the longest x2 6.6 us: carried_in(): return lax.fori_loop(0, count - 1, hop, so_far)]
  transfers between devices with their start and end apart: 2 -> 2, of which waited for: 1 -> 2; matrix products, arithmetic and copies ran while one was open for 1% -> 5% of each run, Pallas kernels for 0% -> 0%
where the time goes in v1:
time: 56.9 us; the launch traced here: 56.3 us
  starting transfers between devices  24.4 us (43%)
  waiting for transfers between devices  16.9 us (30%)
  local copies, waits for them, and re-layouts  7.71 us (14%)
  Pallas kernels  5.34 us (9%)
  other arithmetic  1.28 us (2%)
  between operations  0.66 us (1%)
    all_to_all x1, starting transfers between devices, body(): gathered = lax.all_to_all(spread, 'tm', 0, 0)  16.8 us
    all_to_all x1, waiting for transfers between devices, body(): gathered = lax.all_to_all(spread, 'tm', 0, 0)  10.4 us
    all_to_all x1, starting transfers between devices, body(): parts = lax.all_to_all(sends, 'rows', 0, 0)  7.65 us
    all_to_all x1, waiting for transfers between devices, body(): parts = lax.all_to_all(sends, 'rows', 0, 0)  6.56 us
    unnamed x12, local copies, waits for them, and re-layouts  4.81 us
    pallas_call x1, Pallas kernels, body(): pl.pallas_call(finish_kernel, out_shape=(jax.ShapeDtypeStruct((bars, HALF...  1.96 us
    pallas_call x1, Pallas kernels, body(): pl.pallas_call(block_kernel, out_shape=(jax.ShapeDtypeStruct((5 * count,...  1.83 us
    pallas_call x1, Pallas kernels, body(): pl.pallas_call(project_kernel, out_shape=jax.ShapeDtypeStruct((peers, bar...  1.56 us
  transfers between devices with their start and end apart: 2, of which 2 were waited for; matrix products, arithmetic and copies ran while one was open for 5% of the time, Pallas kernels for 0%

profile of v1, /device:TPU:1, one launch (start us, length us, event | category | flops | bytes accessed | tf_op | source)
XLA Modules:
  0.0 56.3 jit_solution(120671057882238129)
XLA Ops:
  0.6 0.0 copy-start
  0.6 1.0 %copy-done = f32[64,2048]{1,0:T(8,128)S(1)} copy-done((f32[64,2048]{1,0:T(8,128)S(1)}, f32[64,2048]{1,0:T(8,128)}, u32[]{:S(2)}) %copy-start) | copy-done | bytes 524312
  1.7 0.0 copy-start.1
  1.7 1.0 %copy-done.1 = f32[64,2048]{1,0:T(8,128)S(1)} copy-done((f32[64,2048]{1,0:T(8,128)S(1)}, f32[64,2048]{1,0:T(8,128)}, u32[]{:S(2)}) %copy-start.1) | copy-done | bytes 524312
  2.7 0.0 copy-start.2
  2.7 0.7 %copy-done.2 = f32[2048]{0:T(1024)S(1)} copy-done((f32[2048]{0:T(1024)S(1)}, f32[2048]{0:T(1024)}, u32[]{:S(2)}) %copy-start.2) | copy-done | bytes 8216
  3.4 0.0 copy-start.3
  3.4 0.7 %copy-done.3 = s32[2048]{0:T(1024)S(1)} copy-done((s32[2048]{0:T(1024)S(1)}, s32[2048]{0:T(1024)}, u32[]{:S(2)}) %copy-start.3) | copy-done | bytes 8216
  4.1 1.6 %shard_map.77 = f32[8,64,128]{2,1,0:T(8,128)} custom-call(f32[64,2048]{1,0:T(8,128)S(1)} %copy-done, f32[64,2048]{1,0:T(8,128)S(1)} %copy-done.1, f32[1,2048]{1,0:T(1,128)S(1)} %bitcast.6, s32[1,2048]{1,0:T(1,128)S(1)} %bitcast.7), custom_call_target="tpu_custom_call" | custom-call | tf_op jit(solution)/shard_map/pallas_call | solution.py:200
  5.7 7.7 %all-to-all-start = ((f32[8,64,128]{2,1,0:T(8,128)}), f32[8,64,128]{2,1,0:T(8,128)S(1)}, u32[]{:S(2)}, u32[]{:S(2)}) async-start(f32[8,64,128]{2,1,0:T(8,128)} %shard_map.77), calls=%async_computation | async-start | bytes 524288 | tf_op jit(solution)/shard_map/all_to_all | solution.py:212
  13.3 0.8 %dynamic_slice.7 = f32[64]{0:T(128)S(1)} dynamic-slice(f32[512]{0:T(512)} %param.10, s32[]{:T(128)S(6)} %select_n.4), dynamic_slice_sizes={64} | dynamic-slice | bytes 516 | tf_op jit(solution)/shard_map/dynamic_slice | solution.py:210
  14.1 0.6 %maximum_bitcast_fusion.decay_ref = f32[1,128]{1,0:T(1,128)} fusion(f32[64]{0:T(128)S(1)} %dynamic_slice.7), kind=kLoop, calls=%fused_computation.1 | loop fusion | flops 128 | bytes 768 | tf_op jit(solution)/shard_map/broadcast_in_dim | solution.py:211
  14.7 0.8 %constant_dynamic-slice_fusion = (f32[32,64]{1,0:T(8,128)S(1)}, f32[32,64]{1,0:T(8,128)S(1)}) fusion(f32[64,512]{1,0:T(8,128)} %param.11, s32[]{:T(128)S(6)} %select_n.4, s32[]{:T(128)S(6)} %add.5), kind=kLoop, calls=%fused_computation.2 | loop fusion | bytes 32776 | tf_op jit(solution)/shard_map/slice | solution.py:209
  15.5 0.7 %pad_maximum_fusion.noise_ref = f32[32,128]{1,0:T(8,128)} fusion(f32[32,64]{1,0:T(8,128)S(1)} %get-tuple-element.7, f32[32,64]{1,0:T(8,128)S(1)} %get-tuple-element.6), kind=kLoop, calls=%fused_computation | loop fusion | flops 4096 | bytes 32768 | tf_op jit(solution)/shard_map/concatenate | solution.py:209
  16.2 6.6 %all-to-all-done.parts_ref = f32[8,64,128]{2,1,0:T(8,128)S(1)} async-done(((f32[8,64,128]{2,1,0:T(8,128)}), f32[8,64,128]{2,1,0:T(8,128)S(1)}, u32[]{:S(2)}, u32[]{:S(2)}) %all-to-all-start) | async-done | bytes 262176 | tf_op jit(solution)/shard_map/all_to_all | solution.py:212
  22.7 0.0 copy-start.4
  22.7 0.7 %copy-done.4 = f32[8,64,128]{2,1,0:T(8,128)} copy-done((f32[8,64,128]{2,1,0:T(8,128)}, f32[8,64,128]{2,1,0:T(8,128)S(1)}, u32[]{:S(2)}) %copy-start.4) | copy-done | bytes 262168
  23.4 1.8 %shard_map.78 = (f32[45,8,128]{2,1,0:T(8,128)}, f32[4,128]{1,0:T(4,128)}) custom-call(f32[8,64,128]{2,1,0:T(8,128)} %copy-done.4, f32[32,128]{1,0:T(8,128)} %pad_maximum_fusion.noise_ref, f32[1,128]{1,0:T(1,128)} %maximum_bitcast_fusion.decay_ref), custom_call_target="tpu_custom_call" | custom-call | tf_op jit(solution)/shard_map/pallas_call | solution.py:213
  25.3 1.3 %broadcast_in_dim.18 = f32[64,4,128]{2,1,0:T(4,128)} broadcast(f32[4,128]{1,0:T(4,128)} %get-tuple-element.5), dimensions={1,2} | broadcast | bytes 133120 | tf_op jit(solution)/shard_map/broadcast_in_dim | solution.py:222
  26.6 16.8 %all-to-all-start.1 = ((f32[64,4,128]{2,1,0:T(4,128)}), f32[64,4,128]{2,1,0:T(4,128)S(1)}, u32[]{:S(2)}, u32[]{:S(2)}) async-start(f32[64,4,128]{2,1,0:T(4,128)} %broadcast_in_dim.18), calls=%async_computation.1 | async-start | bytes 262144 | tf_op jit(solution)/shard_map/all_to_all | solution.py:223
  43.4 10.4 %all-to-all-done.1 = f32[64,4,128]{2,1,0:T(4,128)S(1)} async-done(((f32[64,4,128]{2,1,0:T(4,128)}), f32[64,4,128]{2,1,0:T(4,128)S(1)}, u32[]{:S(2)}, u32[]{:S(2)}) %all-to-all-start.1) | async-done | bytes 131104 | tf_op jit(solution)/shard_map/all_to_all | solution.py:223
  53.7 0.0 copy-start.5
  53.7 0.6 %copy-done.5 = f32[64,4,128]{2,1,0:T(4,128)} copy-done((f32[64,4,128]{2,1,0:T(4,128)}, f32[64,4,128]{2,1,0:T(4,128)S(1)}, u32[]{:S(2)}) %copy-start.5) | copy-done | bytes 131096
  54.4 2.0 %shard_map.79 = (f32[64,64]{1,0:T(8,128)}, f32[64,64]{1,0:T(8,128)}) custom-call(s32[1]{0:T(128)} %bitcast.place_ref, f32[45,8,128]{2,1,0:T(8,128)} %get-tuple-element.4.local_ref, f32[256,128]{1,0:T(8,128)} %bitcast.8), custom_call_target="tpu_custom_call" | custom-call | tf_op jit(solution)/shard_map/pallas_call | solution.py:225
Async XLA Ops:
  0.6 1.0 %copy-start = (f32[64,2048]{1,0:T(8,128)S(1)}, f32[64,2048]{1,0:T(8,128)}, u32[]{:S(2)}) copy-start(f32[64,2048]{1,0:T(8,128)} %returns_ref.1) | copy-start | bytes 1572868
  1.7 1.0 %copy-start.1 = (f32[64,2048]{1,0:T(8,128)S(1)}, f32[64,2048]{1,0:T(8,128)}, u32[]{:S(2)}) copy-start(f32[64,2048]{1,0:T(8,128)} %variances_ref.1) | copy-start | bytes 1572868
  2.7 0.7 %copy-start.2 = (f32[2048]{0:T(1024)S(1)}, f32[2048]{0:T(1024)}, u32[]{:S(2)}) copy-start(f32[2048]{0:T(1024)} %param.8) | copy-start | bytes 24580
  3.4 0.7 %copy-start.3 = (s32[2048]{0:T(1024)S(1)}, s32[2048]{0:T(1024)}, u32[]{:S(2)}) copy-start(s32[2048]{0:T(1024)} %param.9) | copy-start | bytes 24580
  5.7 17.1 %all-to-all-start = ((f32[8,64,128]{2,1,0:T(8,128)}), f32[8,64,128]{2,1,0:T(8,128)S(1)}, u32[]{:S(2)}, u32[]{:S(2)}) async-start(f32[8,64,128]{2,1,0:T(8,128)} %shard_map.77), calls=%async_computation | async-start | bytes 524288 | tf_op jit(solution)/shard_map/all_to_all | solution.py:212
  22.7 0.7 %copy-start.4 = (f32[8,64,128]{2,1,0:T(8,128)}, f32[8,64,128]{2,1,0:T(8,128)S(1)}, u32[]{:S(2)}) copy-start(f32[8,64,128]{2,1,0:T(8,128)S(1)} %all-to-all-done.parts_ref) | copy-start | bytes 786436
  26.6 27.1 %all-to-all-start.1 = ((f32[64,4,128]{2,1,0:T(4,128)}), f32[64,4,128]{2,1,0:T(4,128)S(1)}, u32[]{:S(2)}, u32[]{:S(2)}) async-start(f32[64,4,128]{2,1,0:T(4,128)} %broadcast_in_dim.18), calls=%async_computation.1 | async-start | bytes 262144 | tf_op jit(solution)/shard_map/all_to_all | solution.py:223
  53.7 0.6 %copy-start.5 = (f32[64,4,128]{2,1,0:T(4,128)}, f32[64,4,128]{2,1,0:T(4,128)S(1)}, u32[]{:S(2)}) copy-start(f32[64,4,128]{2,1,0:T(4,128)S(1)} %all-to-all-done.1) | copy-start | bytes 393220

commit v2 on v1

--- a/solution.py
+++ b/solution.py
@@ -5,7 +5,7 @@
 from jax import lax
 from jax.experimental import pallas as pl
 from jax.experimental.pallas import tpu as pltpu
-from jax.sharding import PartitionSpec as P
+from jax.sharding import Mesh, PartitionSpec as P
 
 SUB = 8
 LANES = 128
@@ -41,17 +41,36 @@
     return lane, sub
 
 
-def project_kernel(returns_ref, variances_ref, loadings_ref, sector_ref, out_ref):
+def project_kernel(
+    returns_hbm, variances_hbm, loadings_hbm, sector_hbm, out_ref,
+    returns_ref, variances_ref, loadings_ref, sector_ref, sems,
+):
     bars, series = returns_ref.shape
     peers = out_ref.shape[0]
     factors = peers * HALF
+    copies = [
+        pltpu.make_async_copy(source, target, sems.at[index])
+        for index, (source, target) in enumerate(
+            (
+                (sector_hbm, sector_ref),
+                (loadings_hbm, loadings_ref),
+                (variances_hbm, variances_ref),
+                (returns_hbm, returns_ref),
+            )
+        )
+    ]
+    for copy in copies:
+        copy.start()
+    copies[0].wait()
+    owner = lax.broadcasted_iota(jnp.int32, (factors, series), 0)
+    one_hot = jnp.where(owner == sector_ref[...], 1.0, 0.0).astype(jnp.bfloat16)
+    for copy in copies[1:]:
+        copy.wait()
     loadings = loadings_ref[...]
     scaled = loadings / variances_ref[...]
     stacked = jnp.concatenate([returns_ref[...] * scaled, scaled * loadings], axis=0)
     upper = stacked.astype(jnp.bfloat16)
     lower = (stacked - upper.astype(jnp.float32)).astype(jnp.bfloat16)
-    owner = lax.broadcasted_iota(jnp.int32, (factors, series), 0)
-    one_hot = jnp.where(owner == sector_ref[...], 1.0, 0.0).astype(jnp.bfloat16)
     both = lax.dot_general(
         jnp.concatenate([upper, lower], axis=0),
         one_hot,
@@ -71,6 +90,18 @@
             out_ref[2 * pair + 1, rows, :] = jnp.where(low_lanes, pltpu.roll(first, HALF, 1), second)
 
 
+def added(terms):
+    while len(terms) > 1:
+        terms = [sum(terms[i + 1 : i + 2], terms[i]) for i in range(0, len(terms), 2)]
+    return terms[0]
+
+
+def spread(ref, rows):
+    tile = jnp.concatenate([*rows, jnp.zeros((SUB - 5, LANES), jnp.float32)], axis=0)
+    for peer in range(ref.shape[0]):
+        ref[peer] = tile
+
+
 def block_kernel(parts_ref, noise_ref, decay_ref, local_ref, summary_ref):
     peers, rows, _ = parts_ref.shape
     half = rows // 2
@@ -79,11 +110,10 @@
     decay = decay_ref[...]
     elements = []
     for step in range(depth):
-        signal = parts_ref[0, pl.ds(step, SUB, stride=depth), :]
-        information = parts_ref[0, pl.ds(half + step, SUB, stride=depth), :]
-        for peer in range(1, peers):
-            signal += parts_ref[peer, pl.ds(step, SUB, stride=depth), :]
-            information += parts_ref[peer, pl.ds(half + step, SUB, stride=depth), :]
+        signal = added([parts_ref[peer, pl.ds(step, SUB, stride=depth), :] for peer in range(peers)])
+        information = added(
+            [parts_ref[peer, pl.ds(half + step, SUB, stride=depth), :] for peer in range(peers)]
+        )
         noise = noise_ref[pl.ds(step, SUB, stride=depth), :]
         inverse = 1.0 / (1.0 + noise * information)
         decayed = decay * inverse
@@ -108,15 +138,9 @@
     before = combine(keep(lane >= HALF, other), keep(sub >= 1, rolled(ahead, 1, 0)))
     after = combine(keep(sub < SUB - 1, rolled(behind, SUB - 1, 0)), keep(lane < HALF, other))
     whole = combine(other, ahead)
-    turned = rolled(whole, HALF, 1)
-    rows_out = (
-        jnp.where(lane < HALF, turned[0], whole[1]),
-        jnp.where(lane < HALF, turned[2], whole[3]),
-        jnp.where(lane < HALF, turned[4], whole[4]),
-    )
-    for row in range(3):
-        summary_ref[row : row + 1, :] = rows_out[row][SUB - 1 :, :]
-    summary_ref[3:4, :] = rows_out[2][SUB - 1 :, :]
+    high = lane[:1, :] >= HALF
+    rows = [part[SUB - 1 :, :] for part in whole]
+    spread(summary_ref, [jnp.where(high, row, pltpu.roll(row, HALF, 1)) for row in rows])
     slot = 0
     for element in (before, after, *forward, *backward[:-1]):
         for part in element:
@@ -124,38 +148,56 @@
             slot += 1
 
 
-def finish_kernel(place_ref, local_ref, gathered_ref, mean_ref, log_ref):
-    blocks = gathered_ref.shape[0] // 4
+def read_rows(ref):
+    return tuple(ref[part : part + 1, :] for part in range(5))
+
+
+def swapped(element, low):
+    mask = lax.broadcasted_iota(jnp.int32, (1, LANES), 1) < HALF
+    turn = rolled(element, HALF, 1)
+    return tuple(
+        jnp.where(mask, own, other) if low else jnp.where(mask, other, own) for own, other in zip(element, turn)
+    )
+
+
+def product(element):
+    for shift in (1, 2, 4):
+        element = combine(element, rolled(element, SUB - shift, 0))
+    return tuple(part[:1, :] for part in element)
+
+
+def received_rows(ref):
+    return tuple(ref[pl.ds(part, SUB, stride=SUB), :] for part in range(5))
+
+
+def around(place, received):
+    lane, sub = iotas()
+    return product(keep(jnp.where(lane < HALF, sub - place, place - sub) < 0, received))
+
+
+def extended(inner, outer):
+    mask = lax.broadcasted_iota(jnp.int32, (1, LANES), 1) < HALF
+    earlier = tuple(jnp.where(mask, o, i) for i, o in zip(inner, outer))
+    later = tuple(jnp.where(mask, i, o) for i, o in zip(inner, outer))
+    return combine(earlier, later)
+
+
+def level_kernel(received_ref, context_ref, total_ref):
+    place = lax.axis_index("near")
+    received = received_rows(received_ref)
+    for part, row in enumerate(around(place, received)):
+        context_ref[part : part + 1, :] = row
+    context_ref[5:, :] = jnp.zeros((SUB - 5, LANES), jnp.float32)
+    spread(total_ref, product(received))
+
+
+def finish_kernel(local_ref, context_ref, received_ref, mean_ref, log_ref):
     depth = (local_ref.shape[0] // 5 - 1) // 2
-    strip = blocks // SUB
-    mine = place_ref[0]
-    lane, sub = iotas()
-    low = lane < HALF
-    pieces = []
-    for step in range(strip):
-        raw = [gathered_ref[pl.ds(4 * step + kind, SUB, stride=4 * strip), :] for kind in range(3)]
-        turn = [pltpu.roll(part, HALF, 1) for part in raw[:2]]
-        element = (
-            jnp.where(low, raw[0], turn[0]),
-            jnp.where(low, turn[0], raw[0]),
-            jnp.where(low, raw[1], turn[1]),
-            jnp.where(low, turn[1], raw[1]),
-            raw[2],
-        )
-        block = sub * strip + step
-        pieces.append(keep(jnp.where(low, block - mine, mine - block) < 0, element))
-    while len(pieces) > 1:
-        pieces = [combine(pieces[i], pieces[i + 1]) for i in range(0, len(pieces), 2)]
-    total = pieces[0]
-    for shift in (1, 2, 4):
-        total = combine(total, rolled(total, SUB - shift, 0))
-    own = [part[:1, :] for part in total]
-    turn = [pltpu.roll(part, HALF, 1) for part in own]
-    low_row = low[:1, :]
-    mean_in = jnp.where(low_row, own[1], turn[1])
-    cov_in = jnp.where(low_row, own[2], turn[2])
-    info_in = jnp.where(low_row, turn[3], own[3])
-    prec_in = jnp.where(low_row, turn[4], own[4])
+    place = lax.axis_index("far")
+    total = extended(read_rows(context_ref), around(place, received_rows(received_ref)))
+    before, after = swapped(total, True), swapped(total, False)
+    mean_in, cov_in = before[1], before[2]
+    info_in, prec_in = after[3], after[4]
 
     def element_at(index):
         return tuple(local_ref[5 * index + part] for part in range(5))
@@ -187,53 +229,71 @@
 
 
 VMEM = pl.BlockSpec(memory_space=pltpu.VMEM)
-SMEM = pl.BlockSpec(memory_space=pltpu.SMEM)
+
+
+SMALL = pltpu.CompilerParams(vmem_limit_bytes=4 * 1024 * 1024)
 
 
 def body(returns, variances, loadings, sector, persistence, factor_noise):
     bars, series = returns.shape
     peers = lax.axis_size("rows")
-    blocks = lax.axis_size("tm")
     half = bars // 2
     depth = half // SUB
     count = 2 * depth + 1
+    row = lax.axis_index("rows")
+    tile = jax.ShapeDtypeStruct((SUB, LANES), jnp.float32)
+    tiles = jax.ShapeDtypeStruct((SUB, SUB, LANES), jnp.float32)
     sends = pl.pallas_call(
         project_kernel,
         out_shape=jax.ShapeDtypeStruct((peers, bars, LANES), jnp.float32),
-        in_specs=[VMEM] * 4,
+        in_specs=[pl.BlockSpec(memory_space=pl.ANY)] * 4,
         out_specs=VMEM,
-        compiler_params=pltpu.CompilerParams(vmem_limit_bytes=32 * 1024 * 1024),
+        scratch_shapes=[
+            pltpu.VMEM((bars, series), jnp.float32),
+            pltpu.VMEM((bars, series), jnp.float32),
+            pltpu.VMEM((1, series), jnp.float32),
+            pltpu.VMEM((1, series), jnp.int32),
+            pltpu.SemaphoreType.DMA((4,)),
+        ],
     )(returns, variances, loadings[None, :], sector[None, :])
-    offset = lax.axis_index("rows") * HALF
+    parts = lax.all_to_all(sends, "rows", 0, 0)
+    offset = row * HALF
     noise = lax.dynamic_slice_in_dim(factor_noise, offset, HALF, 1)
     noise = jnp.concatenate([noise[:half], noise[half:]], axis=1)
     decay = lax.dynamic_slice_in_dim(persistence, offset, HALF, 0)
     decay = jnp.concatenate([decay, decay])[None, :]
-    parts = lax.all_to_all(sends, "rows", 0, 0)
-    local, summary = pl.pallas_call(
+    local, totals = pl.pallas_call(
         block_kernel,
-        out_shape=(
-            jax.ShapeDtypeStruct((5 * count, SUB, LANES), jnp.float32),
-            jax.ShapeDtypeStruct((4, LANES), jnp.float32),
-        ),
+        out_shape=(jax.ShapeDtypeStruct((5 * count, SUB, LANES), jnp.float32), tiles),
         in_specs=[VMEM] * 3,
         out_specs=(VMEM, VMEM),
+        compiler_params=SMALL,
     )(parts, noise, decay)
-    spread = jnp.broadcast_to(summary[None], (blocks, 4, LANES))
-    gathered = lax.all_to_all(spread, "tm", 0, 0)
-    place = jnp.reshape(lax.axis_index("tm"), (1,)).astype(jnp.int32)
+    received = lax.all_to_all(totals, "near", 0, 0)
+    context, totals = pl.pallas_call(
+        level_kernel,
+        out_shape=(tile, tiles),
+        in_specs=[VMEM],
+        out_specs=(VMEM, VMEM),
+        compiler_params=SMALL,
+    )(received.reshape(SUB * SUB, LANES))
+    received = lax.all_to_all(totals, "far", 0, 0)
     return pl.pallas_call(
         finish_kernel,
         out_shape=(
             jax.ShapeDtypeStruct((bars, HALF), jnp.float32),
             jax.ShapeDtypeStruct((bars, HALF), jnp.float32),
         ),
-        in_specs=[SMEM, VMEM, VMEM],
+        in_specs=[VMEM] * 3,
         out_specs=(VMEM, VMEM),
-    )(place, local, gathered.reshape(blocks * 4, LANES))
+        compiler_params=SMALL,
+    )(local, context, received.reshape(SUB * SUB, LANES))
 
 
 def solution(mesh):
-    in_specs = (P("tm", "rows"), P("tm", "rows"), P("rows"), P("rows"), P(), P("tm", None))
-    out_specs = (P("tm", "rows"), P("tm", "rows"))
-    return jax.shard_map(body, mesh=mesh, in_specs=in_specs, out_specs=out_specs, check_vma=False)
+    blocks, peers = mesh.shape["tm"], mesh.shape["rows"]
+    split = Mesh(mesh.devices.reshape(blocks // SUB, SUB, peers), ("far", "near", "rows"))
+    bars = ("far", "near")
+    in_specs = (P(bars, "rows"), P(bars, "rows"), P("rows"), P("rows"), P(), P(bars, None))
+    out_specs = (P(bars, "rows"), P(bars, "rows"))
+    return jax.shard_map(body, mesh=split, in_specs=in_specs, out_specs=out_specs, check_vma=False)

time: 56.9 us -> 56.1 us (0.986)
  blocking collectives: 0 us -> 34 us
  starting transfers between devices: 24.4 us -> 7.66 us
  waiting for transfers between devices: 16.9 us -> 7.69 us
  local copies, waits for them, and re-layouts: 7.71 us -> 1.56 us
  Pallas kernels: 5.34 us -> 3.98 us
  other arithmetic: 1.28 us -> 0.15 us
    all_to_all x0 -> x2, blocking collectives: none -> 34 us  [the longest x1 18.6 us: body(): received = lax.all_to_all(totals, 'far', 0, 0)]
    all_to_all x1 -> x0, starting transfers between devices: 16.8 us -> none  [body(): gathered = lax.all_to_all(spread, 'tm', 0, 0)]
    all_to_all x1 -> x0, waiting for transfers between devices: 10.4 us -> none  [body(): gathered = lax.all_to_all(spread, 'tm', 0, 0)]
    unnamed x12 -> x0, local copies, waits for them, and re-layouts: 4.81 us -> none
    pallas_call x1, Pallas kernels: 1.83 us -> 0.25 us  [body(): pl.pallas_call(block_kernel, out_shape=(jax.ShapeDtypeStruct((5 * count,...]
    broadcast_in_dim x1 -> x0, local copies, waits for them, and re-layouts: 1.33 us -> none  [body(): spread = jnp.broadcast_to(summary[None], (blocks, 4, LANES))]
    pallas_call x1, Pallas kernels: 1.56 us -> 2.81 us  [body(): pl.pallas_call(project_kernel, out_shape=jax.ShapeDtypeStruct((peers, bar...]
    all_to_all x1, waiting for transfers between devices: 6.56 us -> 7.69 us  [body(): parts = lax.all_to_all(sends, 'rows', 0, 0)]
  transfers between devices with their start and end apart: 2 -> 1, of which waited for: 2 -> 1; matrix products, arithmetic and copies ran while one was open for 5% -> 3% of each run, Pallas kernels for 0% -> 0%
where the time goes in v2:
time: 56.1 us; the launch traced here: 55.7 us
  blocking collectives  34 us (61%)
  waiting for transfers between devices  7.69 us (14%)
  starting transfers between devices  7.66 us (14%)
  Pallas kernels  3.98 us (7%)
  local copies, waits for them, and re-layouts  1.56 us (3%)
  between operations  0.66 us (1%)
    all_to_all x1, blocking collectives, body(): received = lax.all_to_all(totals, 'far', 0, 0)  18.6 us
    all_to_all x1, blocking collectives, body(): received = lax.all_to_all(totals, 'near', 0, 0)  15.4 us
    all_to_all x1, waiting for transfers between devices, body(): parts = lax.all_to_all(sends, 'rows', 0, 0)  7.69 us
    all_to_all x1, starting transfers between devices, body(): parts = lax.all_to_all(sends, 'rows', 0, 0)  7.66 us
    pallas_call x1, Pallas kernels, body(): pl.pallas_call(project_kernel, out_shape=jax.ShapeDtypeStruct((peers, bar...  2.81 us
  transfers between devices with their start and end apart: 1, of which 1 were waited for; matrix products, arithmetic and copies ran while one was open for 3% of the time, Pallas kernels for 0%

profile of v2, /device:TPU:1, one launch (start us, length us, event | category | flops | bytes accessed | tf_op | source)
XLA Modules:
  0.0 55.7 jit_solution(6592567803136845628)
XLA Ops:
  0.6 2.8 %shard_map.77 = f32[8,64,128]{2,1,0:T(8,128)} custom-call(f32[64,2048]{1,0:T(8,128)} %returns_hbm.1, f32[64,2048]{1,0:T(8,128)} %variances_hbm.1, f32[1,2048]{1,0:T(1,128)} %bitcast.8, s32[1,2048]{1,0:T(1,128)} %bitcast.9), custom_call_target="tpu_custom_call" | custom-call | tf_op jit(solution)/shard_map/pallas_call | solution.py:246
  3.5 7.7 %all-to-all-start = ((f32[8,64,128]{2,1,0:T(8,128)}), f32[8,64,128]{2,1,0:T(8,128)S(1)}, u32[]{:S(2)}, u32[]{:S(2)}) async-start(f32[8,64,128]{2,1,0:T(8,128)} %shard_map.77), calls=%async_computation | async-start | bytes 524288 | tf_op jit(solution)/shard_map/all_to_all | solution.py:259
  11.1 0.8 %dynamic_slice.7 = f32[64]{0:T(128)S(1)} dynamic-slice(f32[512]{0:T(512)} %param.10, s32[]{:T(128)S(6)} %select_n.4), dynamic_slice_sizes={64} | dynamic-slice | bytes 516 | tf_op jit(solution)/shard_map/dynamic_slice | solution.py:263
  11.9 0.1 maximum_bitcast_fusion.decay_ref
  11.9 0.8 %constant_dynamic-slice_fusion = (f32[32,64]{1,0:T(8,128)S(1)}, f32[32,64]{1,0:T(8,128)S(1)}) fusion(f32[64,512]{1,0:T(8,128)} %param.11, s32[]{:T(128)S(6)} %select_n.4, s32[]{:T(128)S(6)} %add.5), kind=kLoop, calls=%fused_computation.2 | loop fusion | bytes 32776 | tf_op jit(solution)/shard_map/slice | solution.py:262
  12.8 0.1 pad_maximum_fusion.noise_ref
  12.8 7.7 %all-to-all-done.parts_ref = f32[8,64,128]{2,1,0:T(8,128)S(1)} async-done(((f32[8,64,128]{2,1,0:T(8,128)}), f32[8,64,128]{2,1,0:T(8,128)S(1)}, u32[]{:S(2)}, u32[]{:S(2)}) %all-to-all-start) | async-done | bytes 262176 | tf_op jit(solution)/shard_map/all_to_all | solution.py:259
  20.5 0.3 shard_map.78
  20.8 15.4 %all_to_all.15 = f32[8,8,128]{2,1,0:T(8,128)S(1)} all-to-all(f32[8,8,128]{2,1,0:T(8,128)S(1)} %get-tuple-element.7), channel_id=1, replica_groups=mesh['far'=8,'near'=8,'rows'=8] {'near'}, dimensions={0} | all-to-all | bytes 65536 | tf_op jit(solution)/shard_map/all_to_all | solution.py:272
  36.3 18.6 %all_to_all.16 = f32[8,8,128]{2,1,0:T(8,128)S(1)} all-to-all(f32[8,8,128]{2,1,0:T(8,128)S(1)} %get-tuple-element.9), channel_id=1, replica_groups=mesh['far'=8,'near'=8,'rows'=8] {'far'}, dimensions={0} | all-to-all | bytes 65536 | tf_op jit(solution)/shard_map/all_to_all | solution.py:280
  54.9 0.9 %shard_map.80 = (f32[64,64]{1,0:T(8,128)}, f32[64,64]{1,0:T(8,128)}) custom-call(f32[45,8,128]{2,1,0:T(8,128)S(1)} %get-tuple-element.6.local_ref, f32[8,128]{1,0:T(8,128)S(1)} %get-tuple-element.8.context_ref, f32[64,128]{1,0:T(8,128)S(1)} %bitcast.6), custom_call_target="tpu_custom_call" | custom-call | tf_op jit(solution)/shard_map/pallas_call | solution.py:281
  (1 shorter events, 0.0 us)
Async XLA Ops:
  3.5 17.1 %all-to-all-start = ((f32[8,64,128]{2,1,0:T(8,128)}), f32[8,64,128]{2,1,0:T(8,128)S(1)}, u32[]{:S(2)}, u32[]{:S(2)}) async-start(f32[8,64,128]{2,1,0:T(8,128)} %shard_map.77), calls=%async_computation | async-start | bytes 524288 | tf_op jit(solution)/shard_map/all_to_all | solution.py:259

commit v3 on v1

--- a/solution.py
+++ b/solution.py
@@ -10,6 +10,7 @@
 SUB = 8
 LANES = 128
 HALF = 64
+PIECE = 512
 
 
 def combine(earlier, later):
@@ -41,26 +42,61 @@
     return lane, sub
 
 
-def project_kernel(returns_ref, variances_ref, loadings_ref, sector_ref, out_ref):
+def project_kernel(
+    returns_hbm, variances_hbm, loadings_hbm, sector_hbm, noise_hbm, decay_hbm,
+    out_ref, noise_out, decay_out,
+    returns_ref, variances_ref, loadings_ref, sector_ref, noise_ref, decay_ref, sems,
+):
     bars, series = returns_ref.shape
     peers = out_ref.shape[0]
     factors = peers * HALF
-    loadings = loadings_ref[...]
-    scaled = loadings / variances_ref[...]
-    stacked = jnp.concatenate([returns_ref[...] * scaled, scaled * loadings], axis=0)
-    upper = stacked.astype(jnp.bfloat16)
-    lower = (stacked - upper.astype(jnp.float32)).astype(jnp.bfloat16)
-    owner = lax.broadcasted_iota(jnp.int32, (factors, series), 0)
-    one_hot = jnp.where(owner == sector_ref[...], 1.0, 0.0).astype(jnp.bfloat16)
-    both = lax.dot_general(
-        jnp.concatenate([upper, lower], axis=0),
-        one_hot,
-        (((1,), (1,)), ((), ())),
-        preferred_element_type=jnp.float32,
-    )
+    pieces = [slice(first, first + PIECE) for first in range(0, series, PIECE)]
+    moves = [(sector_hbm, sector_ref), (loadings_hbm, loadings_ref)]
+    for piece in pieces:
+        moves.append((variances_hbm.at[:, piece], variances_ref.at[:, piece]))
+        moves.append((returns_hbm.at[:, piece], returns_ref.at[:, piece]))
+    row = lax.axis_index("rows")
+    columns = pl.ds(pl.multiple_of(row // 2 * LANES, LANES), LANES)
+    moves.append((noise_hbm.at[:, columns], noise_ref))
+    moves.append((decay_hbm.at[:, columns], decay_ref))
+    copies = [pltpu.make_async_copy(*move, sems.at[index]) for index, move in enumerate(moves)]
+    for copy in copies:
+        copy.start()
+    copies[0].wait()
+    owner = lax.broadcasted_iota(jnp.int32, (factors, PIECE), 0)
+    one_hot = [
+        jnp.where(owner == sector_ref[:, piece], 1.0, 0.0).astype(jnp.bfloat16) for piece in pieces
+    ]
+    copies[1].wait()
+    both = jnp.zeros((4 * bars, factors), jnp.float32)
+    for index, piece in enumerate(pieces):
+        copies[2 + 2 * index].wait()
+        copies[3 + 2 * index].wait()
+        loadings = loadings_ref[:, piece]
+        scaled = loadings / variances_ref[:, piece]
+        stacked = jnp.concatenate([returns_ref[:, piece] * scaled, scaled * loadings], axis=0)
+        upper = stacked.astype(jnp.bfloat16)
+        lower = (stacked - upper.astype(jnp.float32)).astype(jnp.bfloat16)
+        both += lax.dot_general(
+            jnp.concatenate([upper, lower], axis=0),
+            one_hot[index],
+            (((1,), (1,)), ((), ())),
+            preferred_element_type=jnp.float32,
+        )
     total = both[: 2 * bars] + both[2 * bars :]
     half = bars // 2
     low_lanes = lax.broadcasted_iota(jnp.int32, (half, LANES), 1) < HALF
+    copies[-2].wait()
+    copies[-1].wait()
+    upper_half = jnp.full((half, LANES), row % 2, jnp.int32) == 1
+    early, late = noise_ref[:half, :], noise_ref[half:, :]
+    noise_out[...] = jnp.where(
+        low_lanes,
+        jnp.where(upper_half, pltpu.roll(early, HALF, 1), early),
+        jnp.where(upper_half, late, pltpu.roll(late, HALF, 1)),
+    )
+    decay = decay_ref[...]
+    decay_out[...] = jnp.where(low_lanes[:1] == upper_half[:1], pltpu.roll(decay, HALF, 1), decay)
     for pair in range(factors // LANES):
         columns = slice(pair * LANES, (pair + 1) * LANES)
         for kind in range(2):
@@ -71,7 +107,13 @@
             out_ref[2 * pair + 1, rows, :] = jnp.where(low_lanes, pltpu.roll(first, HALF, 1), second)
 
 
-def block_kernel(parts_ref, noise_ref, decay_ref, local_ref, summary_ref):
+def added(terms):
+    while len(terms) > 1:
+        terms = [sum(terms[i + 1 : i + 2], terms[i]) for i in range(0, len(terms), 2)]
+    return terms[0]
+
+
+def block_kernel(parts_ref, noise_ref, decay_ref, local_ref, summary_hbm, summary_ref, sem):
     peers, rows, _ = parts_ref.shape
     half = rows // 2
     depth = half // SUB
@@ -79,11 +121,10 @@
     decay = decay_ref[...]
     elements = []
     for step in range(depth):
-        signal = parts_ref[0, pl.ds(step, SUB, stride=depth), :]
-        information = parts_ref[0, pl.ds(half + step, SUB, stride=depth), :]
-        for peer in range(1, peers):
-            signal += parts_ref[peer, pl.ds(step, SUB, stride=depth), :]
-            information += parts_ref[peer, pl.ds(half + step, SUB, stride=depth), :]
+        signal = added([parts_ref[peer, pl.ds(step, SUB, stride=depth), :] for peer in range(peers)])
+        information = added(
+            [parts_ref[peer, pl.ds(half + step, SUB, stride=depth), :] for peer in range(peers)]
+        )
         noise = noise_ref[pl.ds(step, SUB, stride=depth), :]
         inverse = 1.0 / (1.0 + noise * information)
         decayed = decay * inverse
@@ -108,32 +149,53 @@
     before = combine(keep(lane >= HALF, other), keep(sub >= 1, rolled(ahead, 1, 0)))
     after = combine(keep(sub < SUB - 1, rolled(behind, SUB - 1, 0)), keep(lane < HALF, other))
     whole = combine(other, ahead)
-    turned = rolled(whole, HALF, 1)
-    rows_out = (
-        jnp.where(lane < HALF, turned[0], whole[1]),
-        jnp.where(lane < HALF, turned[2], whole[3]),
-        jnp.where(lane < HALF, turned[4], whole[4]),
-    )
-    for row in range(3):
-        summary_ref[row : row + 1, :] = rows_out[row][SUB - 1 :, :]
-    summary_ref[3:4, :] = rows_out[2][SUB - 1 :, :]
+    low = lane[:1, :] < HALF
+    rows = [part[SUB - 1 :, :] for part in whole]
+    turned = [pltpu.roll(row, HALF, 1) for row in rows]
+    packed = jnp.concatenate(
+        [
+            jnp.where(low, turned[0], rows[1]),
+            jnp.where(low, turned[2], rows[3]),
+            jnp.where(low, turned[4], rows[4]),
+            jnp.zeros((1, LANES), jnp.float32),
+        ],
+        axis=0,
+    )
+    for peer in range(summary_ref.shape[0]):
+        summary_ref[peer] = packed
+    copy = pltpu.make_async_copy(summary_ref, summary_hbm, sem)
+    copy.start()
     slot = 0
     for element in (before, after, *forward, *backward[:-1]):
         for part in element:
             local_ref[slot] = part
             slot += 1
-
-
-def finish_kernel(place_ref, local_ref, gathered_ref, mean_ref, log_ref):
-    blocks = gathered_ref.shape[0] // 4
+    copy.wait()
+
+
+def swapped(element, low):
+    mask = lax.broadcasted_iota(jnp.int32, (1, LANES), 1) < HALF
+    turn = rolled(element, HALF, 1)
+    return tuple(
+        jnp.where(mask, own, other) if low else jnp.where(mask, other, own) for own, other in zip(element, turn)
+    )
+
+
+def product(element):
+    for shift in (1, 2, 4):
+        element = combine(element, rolled(element, SUB - shift, 0))
+    return tuple(part[:1, :] for part in element)
+
+
+def finish_kernel(local_ref, received_ref, mean_ref, log_ref):
     depth = (local_ref.shape[0] // 5 - 1) // 2
-    strip = blocks // SUB
-    mine = place_ref[0]
+    place = lax.axis_index("tm")
     lane, sub = iotas()
     low = lane < HALF
+    strip = received_ref.shape[0] // (4 * SUB)
     pieces = []
     for step in range(strip):
-        raw = [gathered_ref[pl.ds(4 * step + kind, SUB, stride=4 * strip), :] for kind in range(3)]
+        raw = [received_ref[pl.ds(4 * step + kind, SUB, stride=4 * strip), :] for kind in range(3)]
         turn = [pltpu.roll(part, HALF, 1) for part in raw[:2]]
         element = (
             jnp.where(low, raw[0], turn[0]),
@@ -143,19 +205,13 @@
             raw[2],
         )
         block = sub * strip + step
-        pieces.append(keep(jnp.where(low, block - mine, mine - block) < 0, element))
+        pieces.append(keep(jnp.where(low, block - place, place - block) < 0, element))
     while len(pieces) > 1:
         pieces = [combine(pieces[i], pieces[i + 1]) for i in range(0, len(pieces), 2)]
-    total = pieces[0]
-    for shift in (1, 2, 4):
-        total = combine(total, rolled(total, SUB - shift, 0))
-    own = [part[:1, :] for part in total]
-    turn = [pltpu.roll(part, HALF, 1) for part in own]
-    low_row = low[:1, :]
-    mean_in = jnp.where(low_row, own[1], turn[1])
-    cov_in = jnp.where(low_row, own[2], turn[2])
-    info_in = jnp.where(low_row, turn[3], own[3])
-    prec_in = jnp.where(low_row, turn[4], own[4])
+    total = product(pieces[0])
+    before, after = swapped(total, True), swapped(total, False)
+    mean_in, cov_in = before[1], before[2]
+    info_in, prec_in = after[3], after[4]
 
     def element_at(index):
         return tuple(local_ref[5 * index + part] for part in range(5))
@@ -187,7 +243,9 @@
 
 
 VMEM = pl.BlockSpec(memory_space=pltpu.VMEM)
-SMEM = pl.BlockSpec(memory_space=pltpu.SMEM)
+
+
+SMALL = pltpu.CompilerParams(vmem_limit_bytes=4 * 1024 * 1024)
 
 
 def body(returns, variances, loadings, sector, persistence, factor_noise):
@@ -197,40 +255,55 @@
     half = bars // 2
     depth = half // SUB
     count = 2 * depth + 1
-    sends = pl.pallas_call(
+    inputs = [
+        pltpu.with_memory_space_constraint(array, pltpu.HBM)
+        for array in (
+            returns, variances, loadings[None, :], sector[None, :], factor_noise, persistence[None, :]
+        )
+    ]
+    sends, noise, decay = pl.pallas_call(
         project_kernel,
-        out_shape=jax.ShapeDtypeStruct((peers, bars, LANES), jnp.float32),
-        in_specs=[VMEM] * 4,
-        out_specs=VMEM,
-        compiler_params=pltpu.CompilerParams(vmem_limit_bytes=32 * 1024 * 1024),
-    )(returns, variances, loadings[None, :], sector[None, :])
-    offset = lax.axis_index("rows") * HALF
-    noise = lax.dynamic_slice_in_dim(factor_noise, offset, HALF, 1)
-    noise = jnp.concatenate([noise[:half], noise[half:]], axis=1)
-    decay = lax.dynamic_slice_in_dim(persistence, offset, HALF, 0)
-    decay = jnp.concatenate([decay, decay])[None, :]
+        out_shape=(
+            pltpu.VMEM((peers, bars, LANES), jnp.float32),
+            pltpu.VMEM((half, LANES), jnp.float32),
+            pltpu.VMEM((1, LANES), jnp.float32),
+        ),
+        in_specs=[pl.BlockSpec(memory_space=pltpu.HBM)] * 6,
+        out_specs=(VMEM, VMEM, VMEM),
+        scratch_shapes=[
+            pltpu.VMEM((bars, series), jnp.float32),
+            pltpu.VMEM((bars, series), jnp.float32),
+            pltpu.VMEM((1, series), jnp.float32),
+            pltpu.VMEM((1, series), jnp.int32),
+            pltpu.VMEM((bars, LANES), jnp.float32),
+            pltpu.VMEM((1, LANES), jnp.float32),
+            pltpu.SemaphoreType.DMA((4 + 2 * (series // PIECE),)),
+        ],
+        compiler_params=pltpu.CompilerParams(vmem_limit_bytes=24 * 1024 * 1024),
+    )(*inputs)
     parts = lax.all_to_all(sends, "rows", 0, 0)
     local, summary = pl.pallas_call(
         block_kernel,
         out_shape=(
             jax.ShapeDtypeStruct((5 * count, SUB, LANES), jnp.float32),
-            jax.ShapeDtypeStruct((4, LANES), jnp.float32),
+            jax.ShapeDtypeStruct((blocks, 4, LANES), jnp.float32),
         ),
         in_specs=[VMEM] * 3,
-        out_specs=(VMEM, VMEM),
+        out_specs=(VMEM, pl.BlockSpec(memory_space=pltpu.HBM)),
+        scratch_shapes=[pltpu.VMEM((blocks, 4, LANES), jnp.float32), pltpu.SemaphoreType.DMA],
+        compiler_params=SMALL,
     )(parts, noise, decay)
-    spread = jnp.broadcast_to(summary[None], (blocks, 4, LANES))
-    gathered = lax.all_to_all(spread, "tm", 0, 0)
-    place = jnp.reshape(lax.axis_index("tm"), (1,)).astype(jnp.int32)
+    received = lax.all_to_all(summary, "tm", 0, 0)
     return pl.pallas_call(
         finish_kernel,
         out_shape=(
             jax.ShapeDtypeStruct((bars, HALF), jnp.float32),
             jax.ShapeDtypeStruct((bars, HALF), jnp.float32),
         ),
-        in_specs=[SMEM, VMEM, VMEM],
+        in_specs=[VMEM] * 2,
         out_specs=(VMEM, VMEM),
-    )(place, local, gathered.reshape(blocks * 4, LANES))
+        compiler_params=SMALL,
+    )(local, received.reshape(blocks * 4, LANES))
 
 
 def solution(mesh):

time: 56.9 us -> 48.6 us (0.85)
  blocking collectives: 0 us -> 43.8 us
  starting transfers between devices: 24.4 us -> 0 us
  waiting for transfers between devices: 16.9 us -> 0 us
  local copies, waits for them, and re-layouts: 7.71 us -> 0 us
  Pallas kernels: 5.34 us -> 3.95 us
  other arithmetic: 1.28 us -> 0 us
    all_to_all x0 -> x2, blocking collectives: none -> 43.8 us  [the longest x1 27 us: body(): received = lax.all_to_all(summary, 'tm', 0, 0)]
    all_to_all x2 -> x0, starting transfers between devices: 24.4 us -> none  [the longest x1 16.8 us: body(): gathered = lax.all_to_all(spread, 'tm', 0, 0)]
    all_to_all x2 -> x0, waiting for transfers between devices: 16.9 us -> none  [the longest x1 10.4 us: body(): gathered = lax.all_to_all(spread, 'tm', 0, 0)]
    unnamed x12 -> x0, local copies, waits for them, and re-layouts: 4.81 us -> none
    pallas_call x1, Pallas kernels: 1.83 us -> 0.46 us  [body(): pl.pallas_call(block_kernel, out_shape=(jax.ShapeDtypeStruct((5 * count,...]
    broadcast_in_dim x1 -> x0, local copies, waits for them, and re-layouts: 1.33 us -> none  [body(): spread = jnp.broadcast_to(summary[None], (blocks, 4, LANES))]
    pallas_call x1, Pallas kernels: 1.96 us -> 0.96 us  [body(): pl.pallas_call(finish_kernel, out_shape=(jax.ShapeDtypeStruct((bars, HALF...]
    pallas_call x1, Pallas kernels: 1.56 us -> 2.53 us  [body(): pl.pallas_call(project_kernel, out_shape=(pltpu.VMEM((peers, bars, LANES)...]
  transfers between devices with their start and end apart: 2 -> 0, of which waited for: 2 -> 0; matrix products, arithmetic and copies ran while one was open for 5% -> 0% of each run, Pallas kernels for 0% -> 0%
where the time goes in v3:
time: 48.6 us; the launch traced here: 48.4 us
  blocking collectives  43.8 us (90%)
  Pallas kernels  3.95 us (8%)
  between operations  0.65 us (1%)
    all_to_all x1, blocking collectives, body(): received = lax.all_to_all(summary, 'tm', 0, 0)  27 us
    all_to_all x1, blocking collectives, body(): parts = lax.all_to_all(sends, 'rows', 0, 0)  16.7 us
    pallas_call x1, Pallas kernels, body(): pl.pallas_call(project_kernel, out_shape=(pltpu.VMEM((peers, bars, LANES)...  2.53 us

profile of v3, /device:TPU:1, one launch (start us, length us, event | category | flops | bytes accessed | tf_op | source)
XLA Modules:
  0.0 48.4 jit_solution(16136281011528941775)
XLA Ops:
  0.6 2.5 %shard_map.77 = (f32[8,64,128]{2,1,0:T(8,128)S(1)}, f32[32,128]{1,0:T(8,128)S(1)}, f32[1,128]{1,0:T(1,128)S(1)}) custom-call(f32[64,2048]{1,0:T(8,128)} %returns_hbm.1, f32[64,2048]{1,0:T(8,128)} %variances_hbm.1, f32[1,2048]{1,0:T(1,128)} %bitcast.5, s32[1,2048]{1,0:T(1,128)} %bitcast.6, f32[64,512]{1,0:T(8,128)} %noise_hbm.1, f32[1,512]{1,0:T(1,128)} %bitcast.7), custom_call_target="tpu_custom_call" | custom-call | tf_op jit(solution)/shard_map/pallas_call | solution.py:264
  3.2 16.7 %all_to_all.10.parts_ref = f32[8,64,128]{2,1,0:T(8,128)S(1)} all-to-all(f32[8,64,128]{2,1,0:T(8,128)S(1)} %get-tuple-element.7), channel_id=1, replica_groups=mesh['tm'=64,'rows'=8] {'rows'}, dimensions={0} | all-to-all | bytes 524288 | tf_op jit(solution)/shard_map/all_to_all | solution.py:284
  19.9 0.5 shard_map.78
  20.4 27.0 %all_to_all.11 = f32[64,4,128]{2,1,0:T(4,128)S(1)} all-to-all(f32[64,4,128]{2,1,0:T(4,128)S(1)} %get-tuple-element.11), channel_id=1, replica_groups=mesh['tm'=64,'rows'=8] {'tm'}, dimensions={0} | all-to-all | bytes 262144 | tf_op jit(solution)/shard_map/all_to_all | solution.py:296
  47.4 1.0 %shard_map.79 = (f32[64,64]{1,0:T(8,128)}, f32[64,64]{1,0:T(8,128)}) custom-call(f32[45,8,128]{2,1,0:T(8,128)S(1)} %get-tuple-element.10.local_ref, f32[256,128]{1,0:T(8,128)S(1)} %bitcast.4), custom_call_target="tpu_custom_call" | custom-call | tf_op jit(solution)/shard_map/pallas_call | solution.py:297

commit v4 on v3

--- a/solution.py
+++ b/solution.py
@@ -10,7 +10,9 @@
 SUB = 8
 LANES = 128
 HALF = 64
-PIECE = 512
+PIECE = 1024
+ROW_FIRST = 4
+BLOCK_FIRST = 40
 
 
 def combine(earlier, later):
@@ -103,8 +105,9 @@
             first = total[kind * bars : kind * bars + half, columns]
             second = total[kind * bars + half : (kind + 1) * bars, columns]
             rows = slice(kind * half, (kind + 1) * half)
-            out_ref[2 * pair, rows, :] = jnp.where(low_lanes, first, pltpu.roll(second, HALF, 1))
-            out_ref[2 * pair + 1, rows, :] = jnp.where(low_lanes, pltpu.roll(first, HALF, 1), second)
+            first_slot = (2 * pair - ROW_FIRST) % peers
+            out_ref[first_slot, rows, :] = jnp.where(low_lanes, first, pltpu.roll(second, HALF, 1))
+            out_ref[(first_slot + 1) % peers, rows, :] = jnp.where(low_lanes, pltpu.roll(first, HALF, 1), second)
 
 
 def added(terms):
@@ -195,7 +198,10 @@
     strip = received_ref.shape[0] // (4 * SUB)
     pieces = []
     for step in range(strip):
-        raw = [received_ref[pl.ds(4 * step + kind, SUB, stride=4 * strip), :] for kind in range(3)]
+        raw = [
+            pltpu.roll(received_ref[pl.ds(4 * step + kind, SUB, stride=4 * strip), :], BLOCK_FIRST // SUB, 0)
+            for kind in range(3)
+        ]
         turn = [pltpu.roll(part, HALF, 1) for part in raw[:2]]
         element = (
             jnp.where(low, raw[0], turn[0]),
@@ -246,6 +252,11 @@
 
 
 SMALL = pltpu.CompilerParams(vmem_limit_bytes=4 * 1024 * 1024)
+
+
+def exchanged(x, axis, first):
+    size = lax.axis_size(axis)
+    return lax.all_to_all(x, axis, 0, 0, axis_index_groups=[[(first + i) % size for i in range(size)]])
 
 
 def body(returns, variances, loadings, sector, persistence, factor_noise):
@@ -281,7 +292,7 @@
         ],
         compiler_params=pltpu.CompilerParams(vmem_limit_bytes=24 * 1024 * 1024),
     )(*inputs)
-    parts = lax.all_to_all(sends, "rows", 0, 0)
+    parts = exchanged(sends, "rows", ROW_FIRST)
     local, summary = pl.pallas_call(
         block_kernel,
         out_shape=(
@@ -293,7 +304,7 @@
         scratch_shapes=[pltpu.VMEM((blocks, 4, LANES), jnp.float32), pltpu.SemaphoreType.DMA],
         compiler_params=SMALL,
     )(parts, noise, decay)
-    received = lax.all_to_all(summary, "tm", 0, 0)
+    received = exchanged(summary, "tm", BLOCK_FIRST)
     return pl.pallas_call(
         finish_kernel,
         out_shape=(

time: 48.6 us -> 42.2 us (0.87)
  blocking collectives: 43.8 us -> 37.5 us
    all_to_all x2, blocking collectives: 43.8 us -> 37.5 us  [exchanged(): lax.all_to_all(x, axis, 0, 0, axis_index_groups=[[(first + i) % size for...]
where the time goes in v4:
time: 42.2 us; the launch traced here: 42 us
  blocking collectives  37.5 us (89%)
  Pallas kernels  3.8 us (9%)
  between operations  0.65 us (2%)
    all_to_all x2, blocking collectives, exchanged(): lax.all_to_all(x, axis, 0, 0, axis_index_groups=[[(first + i) % size for...  37.5 us
    pallas_call x1, Pallas kernels, body(): pl.pallas_call(project_kernel, out_shape=(pltpu.VMEM((peers, bars, LANES)...  2.37 us
    pallas_call x1, Pallas kernels, body(): pl.pallas_call(finish_kernel, out_shape=(jax.ShapeDtypeStruct((bars, HALF...  0.97 us

profile of v4, /device:TPU:1, one launch (start us, length us, event | category | flops | bytes accessed | tf_op | source)
XLA Modules:
  0.0 42.0 jit_solution(5607794874520131428)
XLA Ops:
  0.6 2.4 %shard_map.77 = (f32[8,64,128]{2,1,0:T(8,128)S(1)}, f32[32,128]{1,0:T(8,128)S(1)}, f32[1,128]{1,0:T(1,128)S(1)}) custom-call(f32[64,2048]{1,0:T(8,128)} %returns_hbm.1, f32[64,2048]{1,0:T(8,128)} %variances_hbm.1, f32[1,2048]{1,0:T(1,128)} %bitcast.5, s32[1,2048]{1,0:T(1,128)} %bitcast.6, f32[64,512]{1,0:T(8,128)} %noise_hbm.1, f32[1,512]{1,0:T(1,128)} %bitcast.7), custom_call_target="tpu_custom_call" | custom-call | tf_op jit(solution)/shard_map/pallas_call | solution.py:275
  3.0 13.0 %all_to_all.10.parts_ref = f32[8,64,128]{2,1,0:T(8,128)S(1)} all-to-all(f32[8,64,128]{2,1,0:T(8,128)S(1)} %get-tuple-element.7), channel_id=1, replica_groups={{4,5,6,7,0,1,2,3},{12,13,14,15,8,9,10,11},{20,21,22,23,16,17,18,19},{28..., dimensions={0} | all-to-all | bytes 524288 | tf_op jit(solution)/shard_map/all_to_all | solution.py:259
  16.0 0.5 %shard_map.78 = (f32[45,8,128]{2,1,0:T(8,128)S(1)}, f32[64,4,128]{2,1,0:T(4,128)S(1)}) custom-call(f32[8,64,128]{2,1,0:T(8,128)S(1)} %all_to_all.10.parts_ref, f32[32,128]{1,0:T(8,128)S(1)} %get-tuple-element.8.noise_ref, f32[1,128]{1,0:T(1,128)S(1)} %get-tuple-element.9.decay_ref), custom_call_target="tpu_custom_call" | custom-call | tf_op jit(solution)/shard_map/pallas_call | solution.py:296
  16.5 24.5 %all_to_all.11 = f32[64,4,128]{2,1,0:T(4,128)S(1)} all-to-all(f32[64,4,128]{2,1,0:T(4,128)S(1)} %get-tuple-element.11), channel_id=1, replica_groups={{320,328,336,344,352,360,368,376,384,392,400,408,416,424,432,440,448,45..., dimensions={0} | all-to-all | bytes 262144 | tf_op jit(solution)/shard_map/all_to_all | solution.py:259
  41.0 1.0 %shard_map.79 = (f32[64,64]{1,0:T(8,128)}, f32[64,64]{1,0:T(8,128)}) custom-call(f32[45,8,128]{2,1,0:T(8,128)S(1)} %get-tuple-element.10.local_ref, f32[256,128]{1,0:T(8,128)S(1)} %bitcast.4), custom_call_target="tpu_custom_call" | custom-call | tf_op jit(solution)/shard_map/pallas_call | solution.py:308

commit v5 on v3

--- a/solution.py
+++ b/solution.py
@@ -10,7 +10,17 @@
 SUB = 8
 LANES = 128
 HALF = 64
-PIECE = 512
+PIECE = 1024
+
+
+def row_order(peers):
+    first = peers // 2
+    return sorted(range(peers), key=lambda y: (y != first, -min((y - first) % peers, (first - y) % peers), y))
+
+
+def block_order(blocks):
+    first = blocks * 23 // 32
+    return [(first + i) % blocks for i in range(blocks)]
 
 
 def combine(earlier, later):
@@ -97,14 +107,15 @@
     )
     decay = decay_ref[...]
     decay_out[...] = jnp.where(low_lanes[:1] == upper_half[:1], pltpu.roll(decay, HALF, 1), decay)
+    slots = row_order(peers)
     for pair in range(factors // LANES):
         columns = slice(pair * LANES, (pair + 1) * LANES)
         for kind in range(2):
             first = total[kind * bars : kind * bars + half, columns]
             second = total[kind * bars + half : (kind + 1) * bars, columns]
             rows = slice(kind * half, (kind + 1) * half)
-            out_ref[2 * pair, rows, :] = jnp.where(low_lanes, first, pltpu.roll(second, HALF, 1))
-            out_ref[2 * pair + 1, rows, :] = jnp.where(low_lanes, pltpu.roll(first, HALF, 1), second)
+            out_ref[slots.index(2 * pair), rows, :] = jnp.where(low_lanes, first, pltpu.roll(second, HALF, 1))
+            out_ref[slots.index(2 * pair + 1), rows, :] = jnp.where(low_lanes, pltpu.roll(first, HALF, 1), second)
 
 
 def added(terms):
@@ -187,15 +198,17 @@
     return tuple(part[:1, :] for part in element)
 
 
-def finish_kernel(local_ref, received_ref, mean_ref, log_ref):
+def finish_kernel(local_ref, received_ref, mean_ref, log_ref, sorted_ref):
     depth = (local_ref.shape[0] // 5 - 1) // 2
     place = lax.axis_index("tm")
     lane, sub = iotas()
     low = lane < HALF
-    strip = received_ref.shape[0] // (4 * SUB)
+    strip = received_ref.shape[0] // SUB
+    for slot, block in enumerate(block_order(received_ref.shape[0])):
+        sorted_ref[4 * block : 4 * block + 4, :] = received_ref[slot]
     pieces = []
     for step in range(strip):
-        raw = [received_ref[pl.ds(4 * step + kind, SUB, stride=4 * strip), :] for kind in range(3)]
+        raw = [sorted_ref[pl.ds(4 * step + kind, SUB, stride=4 * strip), :] for kind in range(3)]
         turn = [pltpu.roll(part, HALF, 1) for part in raw[:2]]
         element = (
             jnp.where(low, raw[0], turn[0]),
@@ -246,6 +259,10 @@
 
 
 SMALL = pltpu.CompilerParams(vmem_limit_bytes=4 * 1024 * 1024)
+
+
+def exchanged(x, axis, order):
+    return lax.all_to_all(x, axis, 0, 0, axis_index_groups=[order])
 
 
 def body(returns, variances, loadings, sector, persistence, factor_noise):
@@ -281,7 +298,7 @@
         ],
         compiler_params=pltpu.CompilerParams(vmem_limit_bytes=24 * 1024 * 1024),
     )(*inputs)
-    parts = lax.all_to_all(sends, "rows", 0, 0)
+    parts = exchanged(sends, "rows", row_order(peers))
     local, summary = pl.pallas_call(
         block_kernel,
         out_shape=(
@@ -293,7 +310,7 @@
         scratch_shapes=[pltpu.VMEM((blocks, 4, LANES), jnp.float32), pltpu.SemaphoreType.DMA],
         compiler_params=SMALL,
     )(parts, noise, decay)
-    received = lax.all_to_all(summary, "tm", 0, 0)
+    received = exchanged(summary, "tm", block_order(blocks))
     return pl.pallas_call(
         finish_kernel,
         out_shape=(
@@ -302,8 +319,9 @@
         ),
         in_specs=[VMEM] * 2,
         out_specs=(VMEM, VMEM),
+        scratch_shapes=[pltpu.VMEM((blocks * 4, LANES), jnp.float32)],
         compiler_params=SMALL,
-    )(local, received.reshape(blocks * 4, LANES))
+    )(local, received)
 
 
 def solution(mesh):

time: 48.6 us -> 42.2 us (0.87)
  blocking collectives: 43.8 us -> 37.5 us
    all_to_all x2, blocking collectives: 43.8 us -> 37.5 us  [exchanged(): return lax.all_to_all(x, axis, 0, 0, axis_index_groups=[order])]
where the time goes in v5:
time: 42.2 us; the launch traced here: 41.9 us
  blocking collectives  37.5 us (89%)
  Pallas kernels  3.81 us (9%)
  between operations  0.65 us (2%)
    all_to_all x2, blocking collectives, exchanged(): return lax.all_to_all(x, axis, 0, 0, axis_index_groups=[order])  37.5 us
    pallas_call x1, Pallas kernels, body(): pl.pallas_call(project_kernel, out_shape=(pltpu.VMEM((peers, bars, LANES)...  2.37 us
    pallas_call x1, Pallas kernels, body(): pl.pallas_call(finish_kernel, out_shape=(jax.ShapeDtypeStruct((bars, HALF...  0.98 us

profile of v5, /device:TPU:1, one launch (start us, length us, event | category | flops | bytes accessed | tf_op | source)
XLA Modules:
  0.0 41.9 jit_solution(12946958968181085147)
XLA Ops:
  0.6 2.4 %shard_map.77 = (f32[8,64,128]{2,1,0:T(8,128)S(1)}, f32[32,128]{1,0:T(8,128)S(1)}, f32[1,128]{1,0:T(1,128)S(1)}) custom-call(f32[64,2048]{1,0:T(8,128)} %returns_hbm.1, f32[64,2048]{1,0:T(8,128)} %variances_hbm.1, f32[1,2048]{1,0:T(1,128)} %bitcast.3, s32[1,2048]{1,0:T(1,128)} %bitcast.4, f32[64,512]{1,0:T(8,128)} %noise_hbm.1, f32[1,512]{1,0:T(1,128)} %bitcast.5), custom_call_target="tpu_custom_call" | custom-call | tf_op jit(solution)/shard_map/pallas_call | solution.py:281
  3.0 13.0 %all_to_all.10.parts_ref = f32[8,64,128]{2,1,0:T(8,128)S(1)} all-to-all(f32[8,64,128]{2,1,0:T(8,128)S(1)} %get-tuple-element.7), channel_id=1, replica_groups={{4,0,1,7,2,6,3,5},{12,8,9,15,10,14,11,13},{20,16,17,23,18,22,19,21},{28..., dimensions={0} | all-to-all | bytes 524288 | tf_op jit(solution)/shard_map/all_to_all | solution.py:265
  16.0 0.5 %shard_map.78 = (f32[45,8,128]{2,1,0:T(8,128)S(1)}, f32[64,4,128]{2,1,0:T(4,128)S(1)}) custom-call(f32[8,64,128]{2,1,0:T(8,128)S(1)} %all_to_all.10.parts_ref, f32[32,128]{1,0:T(8,128)S(1)} %get-tuple-element.8.noise_ref, f32[1,128]{1,0:T(1,128)S(1)} %get-tuple-element.9.decay_ref), custom_call_target="tpu_custom_call" | custom-call | tf_op jit(solution)/shard_map/pallas_call | solution.py:302
  16.5 24.5 %all_to_all.11.received_ref = f32[64,4,128]{2,1,0:T(4,128)S(1)} all-to-all(f32[64,4,128]{2,1,0:T(4,128)S(1)} %get-tuple-element.11), channel_id=1, replica_groups={{368,376,384,392,400,408,416,424,432,440,448,456,464,472,480,488,496,50..., dimensions={0} | all-to-all | bytes 262144 | tf_op jit(solution)/shard_map/all_to_all | solution.py:265
  41.0 1.0 %shard_map.79 = (f32[64,64]{1,0:T(8,128)}, f32[64,64]{1,0:T(8,128)}) custom-call(f32[45,8,128]{2,1,0:T(8,128)S(1)} %get-tuple-element.10.local_ref, f32[64,4,128]{2,1,0:T(4,128)S(1)} %all_to_all.11.received_ref), custom_call_target="tpu_custom_call" | custom-call | tf_op jit(solution)/shard_map/pallas_call | solution.py:314

commit v6 on v5

--- a/solution.py
+++ b/solution.py
@@ -1,3 +1,5 @@
+import functools
+
 import functools
 
 import jax
@@ -11,6 +13,7 @@
 LANES = 128
 HALF = 64
 PIECE = 1024
+NEAR = 16
 
 
 def row_order(peers):
@@ -18,8 +21,19 @@
     return sorted(range(peers), key=lambda y: (y != first, -min((y - first) % peers, (first - y) % peers), y))
 
 
-def block_order(blocks):
-    first = blocks * 23 // 32
+def near_order(blocks):
+    first = blocks - 2
+    length = max(blocks // 2, 1)
+
+    def far(block):
+        steps = abs(block // 2 - first // 2)
+        return min(steps, length - steps) + block % 2
+
+    return sorted(range(blocks), key=lambda block: (block != first, -far(block), block))
+
+
+def far_order(blocks):
+    first = blocks // 2
     return [(first + i) % blocks for i in range(blocks)]
 
 
@@ -124,7 +138,13 @@
     return terms[0]
 
 
-def block_kernel(parts_ref, noise_ref, decay_ref, local_ref, summary_hbm, summary_ref, sem):
+def spread(ref, rows):
+    tile = jnp.concatenate([*rows, jnp.zeros((SUB - 5, LANES), jnp.float32)], axis=0)
+    for peer in range(ref.shape[0]):
+        ref[peer] = tile
+
+
+def block_kernel(parts_ref, noise_ref, decay_ref, local_ref, summary_ref):
     peers, rows, _ = parts_ref.shape
     half = rows // 2
     depth = half // SUB
@@ -160,28 +180,18 @@
     before = combine(keep(lane >= HALF, other), keep(sub >= 1, rolled(ahead, 1, 0)))
     after = combine(keep(sub < SUB - 1, rolled(behind, SUB - 1, 0)), keep(lane < HALF, other))
     whole = combine(other, ahead)
-    low = lane[:1, :] < HALF
+    high = lane[:1, :] >= HALF
     rows = [part[SUB - 1 :, :] for part in whole]
-    turned = [pltpu.roll(row, HALF, 1) for row in rows]
-    packed = jnp.concatenate(
-        [
-            jnp.where(low, turned[0], rows[1]),
-            jnp.where(low, turned[2], rows[3]),
-            jnp.where(low, turned[4], rows[4]),
-            jnp.zeros((1, LANES), jnp.float32),
-        ],
-        axis=0,
-    )
-    for peer in range(summary_ref.shape[0]):
-        summary_ref[peer] = packed
-    copy = pltpu.make_async_copy(summary_ref, summary_hbm, sem)
-    copy.start()
+    spread(summary_ref, [jnp.where(high, row, pltpu.roll(row, HALF, 1)) for row in rows])
     slot = 0
     for element in (before, after, *forward, *backward[:-1]):
         for part in element:
             local_ref[slot] = part
             slot += 1
-    copy.wait()
+
+
+def read_rows(ref):
+    return tuple(ref[part : part + 1, :] for part in range(5))
 
 
 def swapped(element, low):
@@ -192,36 +202,61 @@
     )
 
 
-def product(element):
+def product(pieces):
+    while len(pieces) > 1:
+        pieces = [combine(pieces[i], pieces[i + 1]) for i in range(0, len(pieces), 2)]
+    total = pieces[0]
     for shift in (1, 2, 4):
-        element = combine(element, rolled(element, SUB - shift, 0))
-    return tuple(part[:1, :] for part in element)
-
-
-def finish_kernel(local_ref, received_ref, mean_ref, log_ref, sorted_ref):
-    depth = (local_ref.shape[0] // 5 - 1) // 2
-    place = lax.axis_index("tm")
-    lane, sub = iotas()
-    low = lane < HALF
-    strip = received_ref.shape[0] // SUB
-    for slot, block in enumerate(block_order(received_ref.shape[0])):
-        sorted_ref[4 * block : 4 * block + 4, :] = received_ref[slot]
+        total = combine(total, rolled(total, SUB - shift, 0))
+    return tuple(part[:1, :] for part in total)
+
+
+def members(received_ref, sorted_ref, order):
+    for slot, member in enumerate(order):
+        sorted_ref[SUB * member : SUB * (member + 1), :] = received_ref[slot]
+    strip = sorted_ref.shape[0] // (SUB * SUB)
+    sub = lax.broadcasted_iota(jnp.int32, (SUB, LANES), 0)
     pieces = []
     for step in range(strip):
-        raw = [sorted_ref[pl.ds(4 * step + kind, SUB, stride=4 * strip), :] for kind in range(3)]
-        turn = [pltpu.roll(part, HALF, 1) for part in raw[:2]]
-        element = (
-            jnp.where(low, raw[0], turn[0]),
-            jnp.where(low, turn[0], raw[0]),
-            jnp.where(low, raw[1], turn[1]),
-            jnp.where(low, turn[1], raw[1]),
-            raw[2],
+        element = tuple(
+            sorted_ref[pl.ds(SUB * step + part, SUB, stride=SUB * strip), :] for part in range(5)
         )
-        block = sub * strip + step
-        pieces.append(keep(jnp.where(low, block - place, place - block) < 0, element))
-    while len(pieces) > 1:
-        pieces = [combine(pieces[i], pieces[i + 1]) for i in range(0, len(pieces), 2)]
-    total = product(pieces[0])
+        pieces.append((sub * strip + step, element))
+    return pieces
+
+
+def around(pieces, place, count):
+    low = lax.broadcasted_iota(jnp.int32, (SUB, LANES), 1) < HALF
+    wanted = []
+    for number, element in pieces:
+        outside = jnp.where(low, number - place, place - number) < 0
+        wanted.append(keep(outside & (number < count), element))
+    return product(wanted)
+
+
+def extended(inner, outer):
+    mask = lax.broadcasted_iota(jnp.int32, (1, LANES), 1) < HALF
+    earlier = tuple(jnp.where(mask, o, i) for i, o in zip(inner, outer))
+    later = tuple(jnp.where(mask, i, o) for i, o in zip(inner, outer))
+    return combine(earlier, later)
+
+
+def level_kernel(received_ref, context_ref, total_ref, sorted_ref):
+    count = received_ref.shape[0]
+    place = lax.rem(lax.axis_index("tm"), count)
+    pieces = members(received_ref, sorted_ref, near_order(count))
+    spread(total_ref, product([keep(number < count, element) for number, element in pieces]))
+    for part, row in enumerate(around(pieces, place, count)):
+        context_ref[part : part + 1, :] = row
+    context_ref[5:, :] = jnp.zeros((SUB - 5, LANES), jnp.float32)
+
+
+def finish_kernel(near, local_ref, context_ref, received_ref, mean_ref, log_ref, sorted_ref):
+    depth = (local_ref.shape[0] // 5 - 1) // 2
+    count = received_ref.shape[0]
+    place = lax.div(lax.axis_index("tm"), near)
+    pieces = members(received_ref, sorted_ref, far_order(count))
+    total = extended(read_rows(context_ref), around(pieces, place, count))
     before, after = swapped(total, True), swapped(total, False)
     mean_in, cov_in = before[1], before[2]
     info_in, prec_in = after[3], after[4]
@@ -261,8 +296,12 @@
 SMALL = pltpu.CompilerParams(vmem_limit_bytes=4 * 1024 * 1024)
 
 
-def exchanged(x, axis, order):
-    return lax.all_to_all(x, axis, 0, 0, axis_index_groups=[order])
+def exchanged(x, axis, groups):
+    return lax.all_to_all(x, axis, 0, 0, axis_index_groups=groups)
+
+
+def sort_scratch(count):
+    return pltpu.VMEM((SUB * max(count, SUB), LANES), jnp.float32)
 
 
 def body(returns, variances, loadings, sector, persistence, factor_noise):
@@ -298,30 +337,45 @@
         ],
         compiler_params=pltpu.CompilerParams(vmem_limit_bytes=24 * 1024 * 1024),
     )(*inputs)
-    parts = exchanged(sends, "rows", row_order(peers))
+    parts = exchanged(sends, "rows", [row_order(peers)])
+    near = min(blocks, NEAR)
+    far = blocks // near
     local, summary = pl.pallas_call(
         block_kernel,
         out_shape=(
             jax.ShapeDtypeStruct((5 * count, SUB, LANES), jnp.float32),
-            jax.ShapeDtypeStruct((blocks, 4, LANES), jnp.float32),
+            jax.ShapeDtypeStruct((near, SUB, LANES), jnp.float32),
         ),
         in_specs=[VMEM] * 3,
-        out_specs=(VMEM, pl.BlockSpec(memory_space=pltpu.HBM)),
-        scratch_shapes=[pltpu.VMEM((blocks, 4, LANES), jnp.float32), pltpu.SemaphoreType.DMA],
+        out_specs=(VMEM, VMEM),
         compiler_params=SMALL,
     )(parts, noise, decay)
-    received = exchanged(summary, "tm", block_order(blocks))
+    groups = [[first + member for member in near_order(near)] for first in range(0, blocks, near)]
+    received = exchanged(summary, "tm", groups)
+    context, summary = pl.pallas_call(
+        level_kernel,
+        out_shape=(
+            jax.ShapeDtypeStruct((SUB, LANES), jnp.float32),
+            jax.ShapeDtypeStruct((far, SUB, LANES), jnp.float32),
+        ),
+        in_specs=[VMEM],
+        out_specs=(VMEM, VMEM),
+        scratch_shapes=[sort_scratch(near)],
+        compiler_params=SMALL,
+    )(received)
+    groups = [[first + near * member for member in far_order(far)] for first in range(near)]
+    received = exchanged(summary, "tm", groups)
     return pl.pallas_call(
-        finish_kernel,
+        functools.partial(finish_kernel, near),
         out_shape=(
             jax.ShapeDtypeStruct((bars, HALF), jnp.float32),
             jax.ShapeDtypeStruct((bars, HALF), jnp.float32),
         ),
-        in_specs=[VMEM] * 2,
+        in_specs=[VMEM] * 3,
         out_specs=(VMEM, VMEM),
-        scratch_shapes=[pltpu.VMEM((blocks * 4, LANES), jnp.float32)],
+        scratch_shapes=[sort_scratch(far)],
         compiler_params=SMALL,
-    )(local, received)
+    )(local, context, received)
 
 
 def solution(mesh):

time: 42.2 us -> 44 us (1.043)
  blocking collectives: 37.5 us -> 39.6 us
    all_to_all x2 -> x3, blocking collectives: 37.5 us -> 39.6 us  [exchanged(): return lax.all_to_all(x, axis, 0, 0, axis_index_groups=groups)]
    pallas_call x1 -> x2, Pallas kernels: 0.98 us -> 0.93 us  [the longest x1 0.87 us: body(): pl.pallas_call(functools.partial(finish_kernel, near), out_shape=(jax.Sha...]
where the time goes in v6:
time: 44 us; the launch traced here: 43.8 us
  blocking collectives  39.6 us (90%)
  Pallas kernels  3.56 us (8%)
  between operations  0.66 us (2%)
    all_to_all x3, blocking collectives, exchanged(): return lax.all_to_all(x, axis, 0, 0, axis_index_groups=groups)  39.6 us
    pallas_call x1, Pallas kernels, body(): pl.pallas_call(project_kernel, out_shape=(pltpu.VMEM((peers, bars, LANES)...  2.37 us

profile of v6, /device:TPU:1, one launch (start us, length us, event | category | flops | bytes accessed | tf_op | source)
XLA Modules:
  0.0 43.8 jit_solution(4003514606562458027)
XLA Ops:
  0.6 2.4 %shard_map.77 = (f32[8,64,128]{2,1,0:T(8,128)S(1)}, f32[32,128]{1,0:T(8,128)S(1)}, f32[1,128]{1,0:T(1,128)S(1)}) custom-call(f32[64,2048]{1,0:T(8,128)} %returns_hbm.1, f32[64,2048]{1,0:T(8,128)} %variances_hbm.1, f32[1,2048]{1,0:T(1,128)} %bitcast.3, s32[1,2048]{1,0:T(1,128)} %bitcast.4, f32[64,512]{1,0:T(8,128)} %noise_hbm.1, f32[1,512]{1,0:T(1,128)} %bitcast.5), custom_call_target="tpu_custom_call" | custom-call | tf_op jit(solution)/shard_map/pallas_call | solution.py:320
  3.0 13.0 %all_to_all.15.parts_ref = f32[8,64,128]{2,1,0:T(8,128)S(1)} all-to-all(f32[8,64,128]{2,1,0:T(8,128)S(1)} %get-tuple-element.9), channel_id=1, replica_groups={{4,0,1,7,2,6,3,5},{12,8,9,15,10,14,11,13},{20,16,17,23,18,22,19,21},{28..., dimensions={0} | all-to-all | bytes 524288 | tf_op jit(solution)/shard_map/all_to_all | solution.py:300
  16.0 0.3 shard_map.78
  16.3 19.7 %all_to_all.16.received_ref = f32[16,8,128]{2,1,0:T(8,128)S(1)} all-to-all(f32[16,8,128]{2,1,0:T(8,128)S(1)} %get-tuple-element.13), channel_id=1, replica_groups={{112,56,40,48,72,24,32,64,88,8,16,80,104,0,96,120},{240,184,168,176,200..., dimensions={0} | all-to-all | bytes 131072 | tf_op jit(solution)/shard_map/all_to_all | solution.py:300
  36.0 0.1 shard_map.79
  36.0 6.9 %all_to_all.17.received_ref = f32[4,8,128]{2,1,0:T(8,128)S(1)} all-to-all(f32[4,8,128]{2,1,0:T(8,128)S(1)} %get-tuple-element.15), channel_id=1, replica_groups={{256,384,0,128},{264,392,8,136},{272,400,16,144},{280,408,24,152},{288,..., dimensions={0} | all-to-all | bytes 32768 | tf_op jit(solution)/shard_map/all_to_all | solution.py:300
  42.9 0.9 %shard_map.80 = (f32[64,64]{1,0:T(8,128)}, f32[64,64]{1,0:T(8,128)}) custom-call(f32[45,8,128]{2,1,0:T(8,128)S(1)} %get-tuple-element.12.local_ref, f32[8,128]{1,0:T(8,128)S(1)} %get-tuple-element.14.context_ref, f32[4,8,128]{2,1,0:T(8,128)S(1)} %all_to_all.17.received_ref), custom_call_target="tpu_custom_call" | custom-call | tf_op jit(solution)/shard_map/pallas_call | solution.py:368

commit v7 on v5

--- a/solution.py
+++ b/solution.py
@@ -20,7 +20,12 @@
 
 def block_order(blocks):
     first = blocks * 23 // 32
-    return [(first + i) % blocks for i in range(blocks)]
+    length = max(blocks // 8, 1)
+
+    def start(block):
+        return block // 2 % length, -(block % 2), block
+
+    return [first] + [block for block in sorted(range(blocks), key=start) if block != first]
 
 
 def combine(earlier, later):
@@ -73,9 +78,11 @@
     for copy in copies:
         copy.start()
     copies[0].wait()
-    owner = lax.broadcasted_iota(jnp.int32, (factors, PIECE), 0)
+    owner = lax.broadcasted_iota(jnp.int16, (factors, PIECE), 0)
+    ones, zeros = jnp.ones(owner.shape, jnp.bfloat16), jnp.zeros(owner.shape, jnp.bfloat16)
     one_hot = [
-        jnp.where(owner == sector_ref[:, piece], 1.0, 0.0).astype(jnp.bfloat16) for piece in pieces
+        jnp.where(owner == jnp.broadcast_to(sector_ref[:, piece].astype(jnp.int16), owner.shape), ones, zeros)
+        for piece in pieces
     ]
     copies[1].wait()
     both = jnp.zeros((4 * bars, factors), jnp.float32)
@@ -124,7 +131,7 @@
     return terms[0]
 
 
-def block_kernel(parts_ref, noise_ref, decay_ref, local_ref, summary_hbm, summary_ref, sem):
+def block_kernel(parts_ref, noise_ref, decay_ref, local_ref, summary_ref):
     peers, rows, _ = parts_ref.shape
     half = rows // 2
     depth = half // SUB
@@ -174,14 +181,11 @@
     )
     for peer in range(summary_ref.shape[0]):
         summary_ref[peer] = packed
-    copy = pltpu.make_async_copy(summary_ref, summary_hbm, sem)
-    copy.start()
     slot = 0
     for element in (before, after, *forward, *backward[:-1]):
         for part in element:
             local_ref[slot] = part
             slot += 1
-    copy.wait()
 
 
 def swapped(element, low):
@@ -306,8 +310,7 @@
             jax.ShapeDtypeStruct((blocks, 4, LANES), jnp.float32),
         ),
         in_specs=[VMEM] * 3,
-        out_specs=(VMEM, pl.BlockSpec(memory_space=pltpu.HBM)),
-        scratch_shapes=[pltpu.VMEM((blocks, 4, LANES), jnp.float32), pltpu.SemaphoreType.DMA],
+        out_specs=(VMEM, VMEM),
         compiler_params=SMALL,
     )(parts, noise, decay)
     received = exchanged(summary, "tm", block_order(blocks))

time: 42.2 us -> 40.9 us (0.969)
  blocking collectives: 37.5 us -> 36.6 us
    all_to_all x2, blocking collectives: 37.5 us -> 36.6 us  [exchanged(): return lax.all_to_all(x, axis, 0, 0, axis_index_groups=[order])]
where the time goes in v7:
time: 40.9 us; the launch traced here: 40.7 us
  blocking collectives  36.6 us (89%)
  Pallas kernels  3.45 us (8%)
  between operations  0.65 us (2%)
    all_to_all x2, blocking collectives, exchanged(): return lax.all_to_all(x, axis, 0, 0, axis_index_groups=[order])  36.6 us
    pallas_call x1, Pallas kernels, body(): pl.pallas_call(project_kernel, out_shape=(pltpu.VMEM((peers, bars, LANES)...  2.19 us
    pallas_call x1, Pallas kernels, body(): pl.pallas_call(finish_kernel, out_shape=(jax.ShapeDtypeStruct((bars, HALF...  0.99 us

profile of v7, /device:TPU:1, one launch (start us, length us, event | category | flops | bytes accessed | tf_op | source)
XLA Modules:
  0.0 40.7 jit_solution(13202418672312592862)
XLA Ops:
  0.6 2.2 %shard_map.77 = (f32[8,64,128]{2,1,0:T(8,128)S(1)}, f32[32,128]{1,0:T(8,128)S(1)}, f32[1,128]{1,0:T(1,128)S(1)}) custom-call(f32[64,2048]{1,0:T(8,128)} %returns_hbm.1, f32[64,2048]{1,0:T(8,128)} %variances_hbm.1, f32[1,2048]{1,0:T(1,128)} %bitcast.3, s32[1,2048]{1,0:T(1,128)} %bitcast.4, f32[64,512]{1,0:T(8,128)} %noise_hbm.1, f32[1,512]{1,0:T(1,128)} %bitcast.5), custom_call_target="tpu_custom_call" | custom-call | tf_op jit(solution)/shard_map/pallas_call | solution.py:285
  2.8 13.0 %all_to_all.10.parts_ref = f32[8,64,128]{2,1,0:T(8,128)S(1)} all-to-all(f32[8,64,128]{2,1,0:T(8,128)S(1)} %get-tuple-element.7), channel_id=1, replica_groups={{4,0,1,7,2,6,3,5},{12,8,9,15,10,14,11,13},{20,16,17,23,18,22,19,21},{28..., dimensions={0} | all-to-all | bytes 524288 | tf_op jit(solution)/shard_map/all_to_all | solution.py:269
  15.9 0.3 shard_map.78
  16.1 23.6 %all_to_all.11.received_ref = f32[64,4,128]{2,1,0:T(4,128)S(1)} all-to-all(f32[64,4,128]{2,1,0:T(4,128)S(1)} %get-tuple-element.11), channel_id=1, replica_groups={{368,8,136,264,392,0,128,256,384,24,152,280,408,16,144,272,400,40,168,2..., dimensions={0} | all-to-all | bytes 262144 | tf_op jit(solution)/shard_map/all_to_all | solution.py:269
  39.7 1.0 %shard_map.79 = (f32[64,64]{1,0:T(8,128)}, f32[64,64]{1,0:T(8,128)}) custom-call(f32[45,8,128]{2,1,0:T(8,128)S(1)} %get-tuple-element.10.local_ref, f32[64,4,128]{2,1,0:T(4,128)S(1)} %all_to_all.11.received_ref), custom_call_target="tpu_custom_call" | custom-call | tf_op jit(solution)/shard_map/pallas_call | solution.py:317

commit v8 on v7

--- a/solution.py
+++ b/solution.py
@@ -10,7 +10,7 @@
 SUB = 8
 LANES = 128
 HALF = 64
-PIECE = 1024
+PIECE = 2048
 
 
 def row_order(peers):
@@ -23,7 +23,8 @@
     length = max(blocks // 8, 1)
 
     def start(block):
-        return block // 2 % length, -(block % 2), block
+        z, x = block // 2 % length, block // 2 // length
+        return z, x in (1, 2), x, -(block % 2)
 
     return [first] + [block for block in sorted(range(blocks), key=start) if block != first]
 

time: 40.9 us -> 41.3 us (level)
  no operation moved by 1% of the time
where the time goes in v8:
time: 41.3 us; the launch traced here: 41 us
  blocking collectives  37 us (90%)
  Pallas kernels  3.44 us (8%)
  between operations  0.65 us (2%)
    all_to_all x2, blocking collectives, exchanged(): return lax.all_to_all(x, axis, 0, 0, axis_index_groups=[order])  37 us
    pallas_call x1, Pallas kernels, body(): pl.pallas_call(project_kernel, out_shape=(pltpu.VMEM((peers, bars, LANES)...  2.18 us
    pallas_call x1, Pallas kernels, body(): pl.pallas_call(finish_kernel, out_shape=(jax.ShapeDtypeStruct((bars, HALF...  0.99 us

profile of v8, /device:TPU:1, one launch (start us, length us, event | category | flops | bytes accessed | tf_op | source)
XLA Modules:
  0.0 41.0 jit_solution(17072434622961359536)
XLA Ops:
  0.6 2.2 %shard_map.77 = (f32[8,64,128]{2,1,0:T(8,128)S(1)}, f32[32,128]{1,0:T(8,128)S(1)}, f32[1,128]{1,0:T(1,128)S(1)}) custom-call(f32[64,2048]{1,0:T(8,128)} %returns_hbm.1, f32[64,2048]{1,0:T(8,128)} %variances_hbm.1, f32[1,2048]{1,0:T(1,128)} %bitcast.3, s32[1,2048]{1,0:T(1,128)} %bitcast.4, f32[64,512]{1,0:T(8,128)} %noise_hbm.1, f32[1,512]{1,0:T(1,128)} %bitcast.5), custom_call_target="tpu_custom_call" | custom-call | tf_op jit(solution)/shard_map/pallas_call | solution.py:286
  2.8 13.0 %all_to_all.10.parts_ref = f32[8,64,128]{2,1,0:T(8,128)S(1)} all-to-all(f32[8,64,128]{2,1,0:T(8,128)S(1)} %get-tuple-element.7), channel_id=1, replica_groups={{4,0,1,7,2,6,3,5},{12,8,9,15,10,14,11,13},{20,16,17,23,18,22,19,21},{28..., dimensions={0} | all-to-all | bytes 524288 | tf_op jit(solution)/shard_map/all_to_all | solution.py:270
  15.8 0.3 shard_map.78
  16.1 23.9 %all_to_all.11.received_ref = f32[64,4,128]{2,1,0:T(4,128)S(1)} all-to-all(f32[64,4,128]{2,1,0:T(4,128)S(1)} %get-tuple-element.11), channel_id=1, replica_groups={{368,8,0,392,384,136,128,264,256,24,16,408,400,152,144,280,272,40,32,42..., dimensions={0} | all-to-all | bytes 262144 | tf_op jit(solution)/shard_map/all_to_all | solution.py:270
  40.0 1.0 %shard_map.79 = (f32[64,64]{1,0:T(8,128)}, f32[64,64]{1,0:T(8,128)}) custom-call(f32[45,8,128]{2,1,0:T(8,128)S(1)} %get-tuple-element.10.local_ref, f32[64,4,128]{2,1,0:T(4,128)S(1)} %all_to_all.11.received_ref), custom_call_target="tpu_custom_call" | custom-call | tf_op jit(solution)/shard_map/pallas_call | solution.py:318

commit v9 on v7

--- a/solution.py
+++ b/solution.py
@@ -18,14 +18,10 @@
     return sorted(range(peers), key=lambda y: (y != first, -min((y - first) % peers, (first - y) % peers), y))
 
 
-def block_order(blocks):
-    first = blocks * 23 // 32
-    length = max(blocks // 8, 1)
-
-    def start(block):
-        return block // 2 % length, -(block % 2), block
-
-    return [first] + [block for block in sorted(range(blocks), key=start) if block != first]
+def chip_order(chips):
+    first = chips * 23 // 32
+    length = max(chips // 4, 1)
+    return [first] + [chip for chip in sorted(range(chips), key=lambda chip: (chip % length, chip)) if chip != first]
 
 
 def combine(earlier, later):
@@ -167,20 +163,11 @@
     before = combine(keep(lane >= HALF, other), keep(sub >= 1, rolled(ahead, 1, 0)))
     after = combine(keep(sub < SUB - 1, rolled(behind, SUB - 1, 0)), keep(lane < HALF, other))
     whole = combine(other, ahead)
-    low = lane[:1, :] < HALF
-    rows = [part[SUB - 1 :, :] for part in whole]
-    turned = [pltpu.roll(row, HALF, 1) for row in rows]
-    packed = jnp.concatenate(
-        [
-            jnp.where(low, turned[0], rows[1]),
-            jnp.where(low, turned[2], rows[3]),
-            jnp.where(low, turned[4], rows[4]),
-            jnp.zeros((1, LANES), jnp.float32),
-        ],
-        axis=0,
-    )
-    for peer in range(summary_ref.shape[0]):
-        summary_ref[peer] = packed
+    high = lane[:1, :] >= HALF
+    for part in range(5):
+        row = whole[part][SUB - 1 :, :]
+        summary_ref[part : part + 1, :] = jnp.where(high, row, pltpu.roll(row, HALF, 1))
+    summary_ref[5:, :] = jnp.zeros((SUB - 5, LANES), jnp.float32)
     slot = 0
     for element in (before, after, *forward, *backward[:-1]):
         for part in element:
@@ -202,13 +189,46 @@
     return tuple(part[:1, :] for part in element)
 
 
-def finish_kernel(local_ref, received_ref, mean_ref, log_ref, sorted_ref):
+def pair_kernel(own_ref, other_ref, context_ref, summary_ref):
+    shape = (1, LANES)
+    low = lax.broadcasted_iota(jnp.int32, shape, 1) < HALF
+    second = jnp.full(shape, lax.rem(lax.axis_index("tm"), 2), jnp.int32) == 1
+    own = tuple(own_ref[part : part + 1, :] for part in range(5))
+    other = tuple(other_ref[part : part + 1, :] for part in range(5))
+    total = combine(
+        tuple(jnp.where(second, b, a) for a, b in zip(own, other)),
+        tuple(jnp.where(second, a, b) for a, b in zip(own, other)),
+    )
+    for part, row in enumerate(keep(low == second, other)):
+        context_ref[part : part + 1, :] = row
+    context_ref[5:, :] = jnp.zeros((SUB - 5, LANES), jnp.float32)
+    packed = jnp.concatenate(
+        [
+            jnp.where(low, total[0], total[1]),
+            jnp.where(low, total[2], total[3]),
+            total[4],
+            jnp.zeros(shape, jnp.float32),
+        ],
+        axis=0,
+    )
+    for peer in range(summary_ref.shape[0]):
+        summary_ref[peer] = packed
+
+
+def extended(inner, outer):
+    mask = lax.broadcasted_iota(jnp.int32, (1, LANES), 1) < HALF
+    earlier = tuple(jnp.where(mask, o, i) for i, o in zip(inner, outer))
+    later = tuple(jnp.where(mask, i, o) for i, o in zip(inner, outer))
+    return combine(earlier, later)
+
+
+def finish_kernel(local_ref, context_ref, received_ref, mean_ref, log_ref, sorted_ref):
     depth = (local_ref.shape[0] // 5 - 1) // 2
-    place = lax.axis_index("tm")
+    place = lax.div(lax.axis_index("tm"), 2)
     lane, sub = iotas()
     low = lane < HALF
     strip = received_ref.shape[0] // SUB
-    for slot, block in enumerate(block_order(received_ref.shape[0])):
+    for slot, block in enumerate(chip_order(received_ref.shape[0])):
         sorted_ref[4 * block : 4 * block + 4, :] = received_ref[slot]
     pieces = []
     for step in range(strip):
@@ -225,7 +245,8 @@
         pieces.append(keep(jnp.where(low, block - place, place - block) < 0, element))
     while len(pieces) > 1:
         pieces = [combine(pieces[i], pieces[i + 1]) for i in range(0, len(pieces), 2)]
-    total = product(pieces[0])
+    context = tuple(context_ref[part : part + 1, :] for part in range(5))
+    total = extended(context, product(pieces[0]))
     before, after = swapped(total, True), swapped(total, False)
     mean_in, cov_in = before[1], before[2]
     info_in, prec_in = after[3], after[4]
@@ -265,8 +286,8 @@
 SMALL = pltpu.CompilerParams(vmem_limit_bytes=4 * 1024 * 1024)
 
 
-def exchanged(x, axis, order):
-    return lax.all_to_all(x, axis, 0, 0, axis_index_groups=[order])
+def exchanged(x, axis, groups):
+    return lax.all_to_all(x, axis, 0, 0, axis_index_groups=groups)
 
 
 def body(returns, variances, loadings, sector, persistence, factor_noise):
@@ -276,6 +297,7 @@
     half = bars // 2
     depth = half // SUB
     count = 2 * depth + 1
+    tile = jax.ShapeDtypeStruct((SUB, LANES), jnp.float32)
     inputs = [
         pltpu.with_memory_space_constraint(array, pltpu.HBM)
         for array in (
@@ -302,29 +324,38 @@
         ],
         compiler_params=pltpu.CompilerParams(vmem_limit_bytes=24 * 1024 * 1024),
     )(*inputs)
-    parts = exchanged(sends, "rows", row_order(peers))
+    parts = exchanged(sends, "rows", [row_order(peers)])
     local, summary = pl.pallas_call(
         block_kernel,
         out_shape=(
             jax.ShapeDtypeStruct((5 * count, SUB, LANES), jnp.float32),
-            jax.ShapeDtypeStruct((blocks, 4, LANES), jnp.float32),
+            tile,
         ),
         in_specs=[VMEM] * 3,
         out_specs=(VMEM, VMEM),
         compiler_params=SMALL,
     )(parts, noise, decay)
-    received = exchanged(summary, "tm", block_order(blocks))
+    other = lax.ppermute(summary, "tm", [(block, block ^ 1) for block in range(blocks)])
+    chips = blocks // 2
+    context, summary = pl.pallas_call(
+        pair_kernel,
+        out_shape=(tile, jax.ShapeDtypeStruct((chips, 4, LANES), jnp.float32)),
+        in_specs=[VMEM] * 2,
+        out_specs=(VMEM, VMEM),
+        compiler_params=SMALL,
+    )(summary, other)
+    received = exchanged(summary, "tm", [[2 * chip + core for chip in chip_order(chips)] for core in range(2)])
     return pl.pallas_call(
         finish_kernel,
         out_shape=(
             jax.ShapeDtypeStruct((bars, HALF), jnp.float32),
             jax.ShapeDtypeStruct((bars, HALF), jnp.float32),
         ),
-        in_specs=[VMEM] * 2,
+        in_specs=[VMEM] * 3,
         out_specs=(VMEM, VMEM),
-        scratch_shapes=[pltpu.VMEM((blocks * 4, LANES), jnp.float32)],
+        scratch_shapes=[pltpu.VMEM((chips * 4, LANES), jnp.float32)],
         compiler_params=SMALL,
-    )(local, received)
+    )(local, context, received)
 
 
 def solution(mesh):

time: 40.9 us -> 42.3 us (1.034)
  starting transfers between devices: 0 us -> 7.67 us
  blocking collectives: 36.6 us -> 29.5 us
  waiting for transfers between devices: 0 us -> 0.8 us
    ppermute x0 -> x1, starting transfers between devices: none -> 7.67 us  [body(): lax.ppermute(summary, 'tm', [(block, block ^ 1) for block in range(blocks)])]
    all_to_all x2, blocking collectives: 36.6 us -> 29.5 us  [exchanged(): return lax.all_to_all(x, axis, 0, 0, axis_index_groups=groups)]
    ppermute x0 -> x1, waiting for transfers between devices: none -> 0.8 us  [body(): lax.ppermute(summary, 'tm', [(block, block ^ 1) for block in range(blocks)])]
  transfers between devices with their start and end apart: 0 -> 1, of which waited for: 0 -> 1; matrix products, arithmetic and copies ran while one was open for 0% -> 0% of each run, Pallas kernels for 0% -> 0%
where the time goes in v9:
time: 42.3 us; the launch traced here: 42 us
  blocking collectives  29.5 us (70%)
  starting transfers between devices  7.67 us (18%)
  Pallas kernels  3.43 us (8%)
  waiting for transfers between devices  0.8 us (2%)
  between operations  0.66 us (2%)
    all_to_all x2, blocking collectives, exchanged(): return lax.all_to_all(x, axis, 0, 0, axis_index_groups=groups)  29.5 us
    ppermute x1, starting transfers between devices, body(): lax.ppermute(summary, 'tm', [(block, block ^ 1) for block in range(blocks)])  7.67 us
    pallas_call x1, Pallas kernels, body(): pl.pallas_call(project_kernel, out_shape=(pltpu.VMEM((peers, bars, LANES)...  2.19 us
    pallas_call x1, Pallas kernels, body(): pl.pallas_call(finish_kernel, out_shape=(jax.ShapeDtypeStruct((bars, HALF...  0.97 us
  transfers between devices with their start and end apart: 1, of which 1 were waited for; matrix products, arithmetic and copies ran while one was open for 0% of the time, Pallas kernels for 0%

profile of v9, /device:TPU:1, one launch (start us, length us, event | category | flops | bytes accessed | tf_op | source)
XLA Modules:
  0.0 42.0 jit_solution(14791487384645840762)
XLA Ops:
  0.6 2.2 %shard_map.77 = (f32[8,64,128]{2,1,0:T(8,128)S(1)}, f32[32,128]{1,0:T(8,128)S(1)}, f32[1,128]{1,0:T(1,128)S(1)}) custom-call(f32[64,2048]{1,0:T(8,128)} %returns_hbm.1, f32[64,2048]{1,0:T(8,128)} %variances_hbm.1, f32[1,2048]{1,0:T(1,128)} %bitcast.3, s32[1,2048]{1,0:T(1,128)} %bitcast.4, f32[64,512]{1,0:T(8,128)} %noise_hbm.1, f32[1,512]{1,0:T(1,128)} %bitcast.5), custom_call_target="tpu_custom_call" | custom-call | tf_op jit(solution)/shard_map/pallas_call | solution.py:307
  2.8 13.0 %all_to_all.10.parts_ref = f32[8,64,128]{2,1,0:T(8,128)S(1)} all-to-all(f32[8,64,128]{2,1,0:T(8,128)S(1)} %get-tuple-element.9), channel_id=1, replica_groups={{4,0,1,7,2,6,3,5},{12,8,9,15,10,14,11,13},{20,16,17,23,18,22,19,21},{28..., dimensions={0} | all-to-all | bytes 524288 | tf_op jit(solution)/shard_map/all_to_all | solution.py:290
  15.9 0.2 shard_map.78
  16.1 7.7 %collective-permute-start = (f32[8,128]{1,0:T(8,128)S(1)}, f32[8,128]{1,0:T(8,128)S(1)}, u32[]{:S(2)}, u32[]{:S(2)}) collective-permute-start(f32[8,128]{1,0:T(8,128)S(1)} %get-tuple-element.13.own_ref), channel_id=1, source_target_pairs={{0,8},{8,0},{16,24},{24,16},{32,40},{40,32},{48,56},{56,48},{64,72... | collective-permute-start | bytes 12296 | tf_op jit(solution)/shard_map/ppermute | solution.py:338
  23.8 0.8 %collective-permute-done.other_ref = f32[8,128]{1,0:T(8,128)S(1)} collective-permute-done((f32[8,128]{1,0:T(8,128)S(1)}, f32[8,128]{1,0:T(8,128)S(1)}, u32[]{:S(2)}, u32[]{:S(2)}) %collective-permute-start) | collective-permute-done | bytes 4128 | tf_op jit(solution)/shard_map/ppermute | solution.py:338
  24.6 16.5 %all_to_all.11.received_ref = f32[32,4,128]{2,1,0:T(4,128)S(1)} all-to-all(f32[32,4,128]{2,1,0:T(4,128)S(1)} %get-tuple-element.15), channel_id=1, replica_groups={{368,0,128,256,384,16,144,272,400,32,160,288,416,48,176,304,432,64,192,..., dimensions={0} | all-to-all | bytes 131072 | tf_op jit(solution)/shard_map/all_to_all | solution.py:290
  41.1 1.0 %shard_map.80 = (f32[64,64]{1,0:T(8,128)}, f32[64,64]{1,0:T(8,128)}) custom-call(f32[45,8,128]{2,1,0:T(8,128)S(1)} %get-tuple-element.12.local_ref, f32[8,128]{1,0:T(8,128)S(1)} %get-tuple-element.14.context_ref, f32[32,4,128]{2,1,0:T(4,128)S(1)} %all_to_all.11.received_ref), custom_call_target="tpu_custom_call" | custom-call | tf_op jit(solution)/shard_map/pallas_call | solution.py:348
  (1 shorter events, 0.0 us)
Async XLA Ops:
  16.1 8.5 %collective-permute-start = (f32[8,128]{1,0:T(8,128)S(1)}, f32[8,128]{1,0:T(8,128)S(1)}, u32[]{:S(2)}, u32[]{:S(2)}) collective-permute-start(f32[8,128]{1,0:T(8,128)S(1)} %get-tuple-element.13.own_ref), channel_id=1, source_target_pairs={{0,8},{8,0},{16,24},{24,16},{32,40},{40,32},{48,56},{56,48},{64,72... | collective-permute-start | bytes 12296 | tf_op jit(solution)/shard_map/ppermute | solution.py:338

commit v10 on v7

--- a/solution.py
+++ b/solution.py
@@ -10,7 +10,6 @@
 SUB = 8
 LANES = 128
 HALF = 64
-PIECE = 1024
 
 
 def row_order(peers):
@@ -65,11 +64,12 @@
     bars, series = returns_ref.shape
     peers = out_ref.shape[0]
     factors = peers * HALF
-    pieces = [slice(first, first + PIECE) for first in range(0, series, PIECE)]
+    half = bars // 2
     moves = [(sector_hbm, sector_ref), (loadings_hbm, loadings_ref)]
+    pieces = [slice(0, half), slice(half, bars)]
     for piece in pieces:
-        moves.append((variances_hbm.at[:, piece], variances_ref.at[:, piece]))
-        moves.append((returns_hbm.at[:, piece], returns_ref.at[:, piece]))
+        moves.append((variances_hbm.at[piece, :], variances_ref.at[piece, :]))
+        moves.append((returns_hbm.at[piece, :], returns_ref.at[piece, :]))
     row = lax.axis_index("rows")
     columns = pl.ds(pl.multiple_of(row // 2 * LANES, LANES), LANES)
     moves.append((noise_hbm.at[:, columns], noise_ref))
@@ -78,30 +78,28 @@
     for copy in copies:
         copy.start()
     copies[0].wait()
-    owner = lax.broadcasted_iota(jnp.int16, (factors, PIECE), 0)
+    owner = lax.broadcasted_iota(jnp.int16, (factors, series), 0)
     ones, zeros = jnp.ones(owner.shape, jnp.bfloat16), jnp.zeros(owner.shape, jnp.bfloat16)
-    one_hot = [
-        jnp.where(owner == jnp.broadcast_to(sector_ref[:, piece].astype(jnp.int16), owner.shape), ones, zeros)
-        for piece in pieces
-    ]
+    one_hot = jnp.where(
+        owner == jnp.broadcast_to(sector_ref[...].astype(jnp.int16), owner.shape), ones, zeros
+    )
     copies[1].wait()
-    both = jnp.zeros((4 * bars, factors), jnp.float32)
+    loadings = loadings_ref[...]
+    totals = []
     for index, piece in enumerate(pieces):
         copies[2 + 2 * index].wait()
         copies[3 + 2 * index].wait()
-        loadings = loadings_ref[:, piece]
-        scaled = loadings / variances_ref[:, piece]
-        stacked = jnp.concatenate([returns_ref[:, piece] * scaled, scaled * loadings], axis=0)
+        scaled = loadings / variances_ref[piece, :]
+        stacked = jnp.concatenate([returns_ref[piece, :] * scaled, scaled * loadings], axis=0)
         upper = stacked.astype(jnp.bfloat16)
         lower = (stacked - upper.astype(jnp.float32)).astype(jnp.bfloat16)
-        both += lax.dot_general(
+        both = lax.dot_general(
             jnp.concatenate([upper, lower], axis=0),
-            one_hot[index],
+            one_hot,
             (((1,), (1,)), ((), ())),
             preferred_element_type=jnp.float32,
         )
-    total = both[: 2 * bars] + both[2 * bars :]
-    half = bars // 2
+        totals.append(both[:bars] + both[bars:])
     low_lanes = lax.broadcasted_iota(jnp.int32, (half, LANES), 1) < HALF
     copies[-2].wait()
     copies[-1].wait()
@@ -118,9 +116,8 @@
     for pair in range(factors // LANES):
         columns = slice(pair * LANES, (pair + 1) * LANES)
         for kind in range(2):
-            first = total[kind * bars : kind * bars + half, columns]
-            second = total[kind * bars + half : (kind + 1) * bars, columns]
             rows = slice(kind * half, (kind + 1) * half)
+            first, second = (total[rows, columns] for total in totals)
             out_ref[slots.index(2 * pair), rows, :] = jnp.where(low_lanes, first, pltpu.roll(second, HALF, 1))
             out_ref[slots.index(2 * pair + 1), rows, :] = jnp.where(low_lanes, pltpu.roll(first, HALF, 1), second)
 
@@ -298,7 +295,7 @@
             pltpu.VMEM((1, series), jnp.int32),
             pltpu.VMEM((bars, LANES), jnp.float32),
             pltpu.VMEM((1, LANES), jnp.float32),
-            pltpu.SemaphoreType.DMA((4 + 2 * (series // PIECE),)),
+            pltpu.SemaphoreType.DMA((8,)),
         ],
         compiler_params=pltpu.CompilerParams(vmem_limit_bytes=24 * 1024 * 1024),
     )(*inputs)

time: 40.9 us -> 41.7 us (1.020)
  Pallas kernels: 3.45 us -> 4.18 us
    pallas_call x1, Pallas kernels: 2.19 us -> 2.93 us  [body(): pl.pallas_call(project_kernel, out_shape=(pltpu.VMEM((peers, bars, LANES)...]
where the time goes in v10:
time: 41.7 us; the launch traced here: 41.4 us
  blocking collectives  36.6 us (88%)
  Pallas kernels  4.18 us (10%)
  between operations  0.65 us (2%)
    all_to_all x2, blocking collectives, exchanged(): return lax.all_to_all(x, axis, 0, 0, axis_index_groups=[order])  36.6 us
    pallas_call x1, Pallas kernels, body(): pl.pallas_call(project_kernel, out_shape=(pltpu.VMEM((peers, bars, LANES)...  2.93 us
    pallas_call x1, Pallas kernels, body(): pl.pallas_call(finish_kernel, out_shape=(jax.ShapeDtypeStruct((bars, HALF...  0.99 us

profile of v10, /device:TPU:1, one launch (start us, length us, event | category | flops | bytes accessed | tf_op | source)
XLA Modules:
  0.0 41.4 jit_solution(5522883812220133879)
XLA Ops:
  0.6 2.9 %shard_map.77 = (f32[8,64,128]{2,1,0:T(8,128)S(1)}, f32[32,128]{1,0:T(8,128)S(1)}, f32[1,128]{1,0:T(1,128)S(1)}) custom-call(f32[64,2048]{1,0:T(8,128)} %returns_hbm.1, f32[64,2048]{1,0:T(8,128)} %variances_hbm.1, f32[1,2048]{1,0:T(1,128)} %bitcast.3, s32[1,2048]{1,0:T(1,128)} %bitcast.4, f32[64,512]{1,0:T(8,128)} %noise_hbm.1, f32[1,512]{1,0:T(1,128)} %bitcast.5), custom_call_target="tpu_custom_call" | custom-call | tf_op jit(solution)/shard_map/pallas_call | solution.py:282
  3.6 13.0 %all_to_all.10.parts_ref = f32[8,64,128]{2,1,0:T(8,128)S(1)} all-to-all(f32[8,64,128]{2,1,0:T(8,128)S(1)} %get-tuple-element.7), channel_id=1, replica_groups={{4,0,1,7,2,6,3,5},{12,8,9,15,10,14,11,13},{20,16,17,23,18,22,19,21},{28..., dimensions={0} | all-to-all | bytes 524288 | tf_op jit(solution)/shard_map/all_to_all | solution.py:266
  16.6 0.3 shard_map.78
  16.9 23.6 %all_to_all.11.received_ref = f32[64,4,128]{2,1,0:T(4,128)S(1)} all-to-all(f32[64,4,128]{2,1,0:T(4,128)S(1)} %get-tuple-element.11), channel_id=1, replica_groups={{368,8,136,264,392,0,128,256,384,24,152,280,408,16,144,272,400,40,168,2..., dimensions={0} | all-to-all | bytes 262144 | tf_op jit(solution)/shard_map/all_to_all | solution.py:266
  40.4 1.0 %shard_map.79 = (f32[64,64]{1,0:T(8,128)}, f32[64,64]{1,0:T(8,128)}) custom-call(f32[45,8,128]{2,1,0:T(8,128)S(1)} %get-tuple-element.10.local_ref, f32[64,4,128]{2,1,0:T(4,128)S(1)} %all_to_all.11.received_ref), custom_call_target="tpu_custom_call" | custom-call | tf_op jit(solution)/shard_map/pallas_call | solution.py:314

commit v11 on v7

--- a/solution.py
+++ b/solution.py
@@ -78,11 +78,17 @@
     for copy in copies:
         copy.start()
     copies[0].wait()
-    owner = lax.broadcasted_iota(jnp.int16, (factors, PIECE), 0)
+    owner = lax.broadcasted_iota(jnp.int16, (LANES, factors), 1)
     ones, zeros = jnp.ones(owner.shape, jnp.bfloat16), jnp.zeros(owner.shape, jnp.bfloat16)
+    strips = []
+    for first in range(0, series, LANES):
+        across = jnp.broadcast_to(sector_ref[:, first : first + LANES], (LANES, LANES))
+        down = across.T.astype(jnp.int16)
+        strips.append(jnp.where(owner == jnp.concatenate([down] * (factors // LANES), axis=1), ones, zeros))
+    per_piece = PIECE // LANES
     one_hot = [
-        jnp.where(owner == jnp.broadcast_to(sector_ref[:, piece].astype(jnp.int16), owner.shape), ones, zeros)
-        for piece in pieces
+        jnp.concatenate(strips[first : first + per_piece], axis=0)
+        for first in range(0, len(strips), per_piece)
     ]
     copies[1].wait()
     both = jnp.zeros((4 * bars, factors), jnp.float32)
@@ -97,7 +103,7 @@
         both += lax.dot_general(
             jnp.concatenate([upper, lower], axis=0),
             one_hot[index],
-            (((1,), (1,)), ((), ())),
+            (((1,), (0,)), ((), ())),
             preferred_element_type=jnp.float32,
         )
     total = both[: 2 * bars] + both[2 * bars :]

time: 40.9 us -> 40.9 us (level)
  no operation moved by 1% of the time
where the time goes in v11:
time: 40.9 us; the launch traced here: 40.7 us
  blocking collectives  36.6 us (89%)
  Pallas kernels  3.41 us (8%)
  between operations  0.65 us (2%)
    all_to_all x2, blocking collectives, exchanged(): return lax.all_to_all(x, axis, 0, 0, axis_index_groups=[order])  36.6 us
    pallas_call x1, Pallas kernels, body(): pl.pallas_call(project_kernel, out_shape=(pltpu.VMEM((peers, bars, LANES)...  2.15 us
    pallas_call x1, Pallas kernels, body(): pl.pallas_call(finish_kernel, out_shape=(jax.ShapeDtypeStruct((bars, HALF...  0.99 us

profile of v11, /device:TPU:1, one launch (start us, length us, event | category | flops | bytes accessed | tf_op | source)
XLA Modules:
  0.0 40.7 jit_solution(8351055870482834520)
XLA Ops:
  0.6 2.2 %shard_map.77 = (f32[8,64,128]{2,1,0:T(8,128)S(1)}, f32[32,128]{1,0:T(8,128)S(1)}, f32[1,128]{1,0:T(1,128)S(1)}) custom-call(f32[64,2048]{1,0:T(8,128)} %returns_hbm.1, f32[64,2048]{1,0:T(8,128)} %variances_hbm.1, f32[1,2048]{1,0:T(1,128)} %bitcast.3, s32[1,2048]{1,0:T(1,128)} %bitcast.4, f32[64,512]{1,0:T(8,128)} %noise_hbm.1, f32[1,512]{1,0:T(1,128)} %bitcast.5), custom_call_target="tpu_custom_call" | custom-call | tf_op jit(solution)/shard_map/pallas_call | solution.py:291
  2.8 13.0 %all_to_all.10.parts_ref = f32[8,64,128]{2,1,0:T(8,128)S(1)} all-to-all(f32[8,64,128]{2,1,0:T(8,128)S(1)} %get-tuple-element.7), channel_id=1, replica_groups={{4,0,1,7,2,6,3,5},{12,8,9,15,10,14,11,13},{20,16,17,23,18,22,19,21},{28..., dimensions={0} | all-to-all | bytes 524288 | tf_op jit(solution)/shard_map/all_to_all | solution.py:275
  15.8 0.3 shard_map.78
  16.1 23.6 %all_to_all.11.received_ref = f32[64,4,128]{2,1,0:T(4,128)S(1)} all-to-all(f32[64,4,128]{2,1,0:T(4,128)S(1)} %get-tuple-element.11), channel_id=1, replica_groups={{368,8,136,264,392,0,128,256,384,24,152,280,408,16,144,272,400,40,168,2..., dimensions={0} | all-to-all | bytes 262144 | tf_op jit(solution)/shard_map/all_to_all | solution.py:275
  39.7 1.0 %shard_map.79 = (f32[64,64]{1,0:T(8,128)}, f32[64,64]{1,0:T(8,128)}) custom-call(f32[45,8,128]{2,1,0:T(8,128)S(1)} %get-tuple-element.10.local_ref, f32[64,4,128]{2,1,0:T(4,128)S(1)} %all_to_all.11.received_ref), custom_call_target="tpu_custom_call" | custom-call | tf_op jit(solution)/shard_map/pallas_call | solution.py:323

commit v12 on v7

--- a/solution.py
+++ b/solution.py
@@ -85,7 +85,7 @@
         for piece in pieces
     ]
     copies[1].wait()
-    both = jnp.zeros((4 * bars, factors), jnp.float32)
+    both = jnp.zeros((factors, 4 * bars), jnp.float32)
     for index, piece in enumerate(pieces):
         copies[2 + 2 * index].wait()
         copies[3 + 2 * index].wait()
@@ -95,12 +95,12 @@
         upper = stacked.astype(jnp.bfloat16)
         lower = (stacked - upper.astype(jnp.float32)).astype(jnp.bfloat16)
         both += lax.dot_general(
+            one_hot[index],
             jnp.concatenate([upper, lower], axis=0),
-            one_hot[index],
             (((1,), (1,)), ((), ())),
             preferred_element_type=jnp.float32,
         )
-    total = both[: 2 * bars] + both[2 * bars :]
+    across = both[:, : 2 * bars] + both[:, 2 * bars :]
     half = bars // 2
     low_lanes = lax.broadcasted_iota(jnp.int32, (half, LANES), 1) < HALF
     copies[-2].wait()
@@ -116,10 +116,10 @@
     decay_out[...] = jnp.where(low_lanes[:1] == upper_half[:1], pltpu.roll(decay, HALF, 1), decay)
     slots = row_order(peers)
     for pair in range(factors // LANES):
-        columns = slice(pair * LANES, (pair + 1) * LANES)
+        total = across[pair * LANES : (pair + 1) * LANES].T
         for kind in range(2):
-            first = total[kind * bars : kind * bars + half, columns]
-            second = total[kind * bars + half : (kind + 1) * bars, columns]
+            first = total[kind * bars : kind * bars + half]
+            second = total[kind * bars + half : (kind + 1) * bars]
             rows = slice(kind * half, (kind + 1) * half)
             out_ref[slots.index(2 * pair), rows, :] = jnp.where(low_lanes, first, pltpu.roll(second, HALF, 1))
             out_ref[slots.index(2 * pair + 1), rows, :] = jnp.where(low_lanes, pltpu.roll(first, HALF, 1), second)

time: 40.9 us -> 41 us (level)
  no operation moved by 1% of the time
where the time goes in v12:
time: 41 us; the launch traced here: 40.8 us
  blocking collectives  36.6 us (89%)
  Pallas kernels  3.52 us (9%)
  between operations  0.65 us (2%)
    all_to_all x2, blocking collectives, exchanged(): return lax.all_to_all(x, axis, 0, 0, axis_index_groups=[order])  36.6 us
    pallas_call x1, Pallas kernels, body(): pl.pallas_call(project_kernel, out_shape=(pltpu.VMEM((peers, bars, LANES)...  2.26 us
    pallas_call x1, Pallas kernels, body(): pl.pallas_call(finish_kernel, out_shape=(jax.ShapeDtypeStruct((bars, HALF...  0.99 us

profile of v12, /device:TPU:1, one launch (start us, length us, event | category | flops | bytes accessed | tf_op | source)
XLA Modules:
  0.0 40.8 jit_solution(11522043478699406260)
XLA Ops:
  0.6 2.3 %shard_map.77 = (f32[8,64,128]{2,1,0:T(8,128)S(1)}, f32[32,128]{1,0:T(8,128)S(1)}, f32[1,128]{1,0:T(1,128)S(1)}) custom-call(f32[64,2048]{1,0:T(8,128)} %returns_hbm.1, f32[64,2048]{1,0:T(8,128)} %variances_hbm.1, f32[1,2048]{1,0:T(1,128)} %bitcast.3, s32[1,2048]{1,0:T(1,128)} %bitcast.4, f32[64,512]{1,0:T(8,128)} %noise_hbm.1, f32[1,512]{1,0:T(1,128)} %bitcast.5), custom_call_target="tpu_custom_call" | custom-call | tf_op jit(solution)/shard_map/pallas_call | solution.py:285
  2.9 13.0 %all_to_all.10.parts_ref = f32[8,64,128]{2,1,0:T(8,128)S(1)} all-to-all(f32[8,64,128]{2,1,0:T(8,128)S(1)} %get-tuple-element.7), channel_id=1, replica_groups={{4,0,1,7,2,6,3,5},{12,8,9,15,10,14,11,13},{20,16,17,23,18,22,19,21},{28..., dimensions={0} | all-to-all | bytes 524288 | tf_op jit(solution)/shard_map/all_to_all | solution.py:269
  15.9 0.3 shard_map.78
  16.2 23.6 %all_to_all.11.received_ref = f32[64,4,128]{2,1,0:T(4,128)S(1)} all-to-all(f32[64,4,128]{2,1,0:T(4,128)S(1)} %get-tuple-element.11), channel_id=1, replica_groups={{368,8,136,264,392,0,128,256,384,24,152,280,408,16,144,272,400,40,168,2..., dimensions={0} | all-to-all | bytes 262144 | tf_op jit(solution)/shard_map/all_to_all | solution.py:269
  39.8 1.0 %shard_map.79 = (f32[64,64]{1,0:T(8,128)}, f32[64,64]{1,0:T(8,128)}) custom-call(f32[45,8,128]{2,1,0:T(8,128)S(1)} %get-tuple-element.10.local_ref, f32[64,4,128]{2,1,0:T(4,128)S(1)} %all_to_all.11.received_ref), custom_call_target="tpu_custom_call" | custom-call | tf_op jit(solution)/shard_map/pallas_call | solution.py:317

commit v13 on v7

--- a/solution.py
+++ b/solution.py
@@ -15,7 +15,7 @@
 
 def row_order(peers):
     first = peers // 2
-    return sorted(range(peers), key=lambda y: (y != first, -min((y - first) % peers, (first - y) % peers), y))
+    return sorted(range(peers), key=lambda y: (y != first, min((y - first) % peers, (first - y) % peers), y))
 
 
 def block_order(blocks):

time: 40.9 us -> 40.9 us (level)
  no operation moved by 1% of the time
where the time goes in v13:
time: 40.9 us; the launch traced here: 40.7 us
  blocking collectives  36.6 us (89%)
  Pallas kernels  3.45 us (8%)
  between operations  0.65 us (2%)
    all_to_all x2, blocking collectives, exchanged(): return lax.all_to_all(x, axis, 0, 0, axis_index_groups=[order])  36.6 us
    pallas_call x1, Pallas kernels, body(): pl.pallas_call(project_kernel, out_shape=(pltpu.VMEM((peers, bars, LANES)...  2.19 us
    pallas_call x1, Pallas kernels, body(): pl.pallas_call(finish_kernel, out_shape=(jax.ShapeDtypeStruct((bars, HALF...  0.99 us

profile of v13, /device:TPU:1, one launch (start us, length us, event | category | flops | bytes accessed | tf_op | source)
XLA Modules:
  0.0 40.7 jit_solution(16428104564596024716)
XLA Ops:
  0.6 2.2 %shard_map.77 = (f32[8,64,128]{2,1,0:T(8,128)S(1)}, f32[32,128]{1,0:T(8,128)S(1)}, f32[1,128]{1,0:T(1,128)S(1)}) custom-call(f32[64,2048]{1,0:T(8,128)} %returns_hbm.1, f32[64,2048]{1,0:T(8,128)} %variances_hbm.1, f32[1,2048]{1,0:T(1,128)} %bitcast.3, s32[1,2048]{1,0:T(1,128)} %bitcast.4, f32[64,512]{1,0:T(8,128)} %noise_hbm.1, f32[1,512]{1,0:T(1,128)} %bitcast.5), custom_call_target="tpu_custom_call" | custom-call | tf_op jit(solution)/shard_map/pallas_call | solution.py:285
  2.8 13.0 %all_to_all.10.parts_ref = f32[8,64,128]{2,1,0:T(8,128)S(1)} all-to-all(f32[8,64,128]{2,1,0:T(8,128)S(1)} %get-tuple-element.7), channel_id=1, replica_groups={{4,3,5,2,6,1,7,0},{12,11,13,10,14,9,15,8},{20,19,21,18,22,17,23,16},{28..., dimensions={0} | all-to-all | bytes 524288 | tf_op jit(solution)/shard_map/all_to_all | solution.py:269
  15.8 0.3 shard_map.78
  16.1 23.6 %all_to_all.11.received_ref = f32[64,4,128]{2,1,0:T(4,128)S(1)} all-to-all(f32[64,4,128]{2,1,0:T(4,128)S(1)} %get-tuple-element.11), channel_id=1, replica_groups={{368,8,136,264,392,0,128,256,384,24,152,280,408,16,144,272,400,40,168,2..., dimensions={0} | all-to-all | bytes 262144 | tf_op jit(solution)/shard_map/all_to_all | solution.py:269
  39.7 1.0 %shard_map.79 = (f32[64,64]{1,0:T(8,128)}, f32[64,64]{1,0:T(8,128)}) custom-call(f32[45,8,128]{2,1,0:T(8,128)S(1)} %get-tuple-element.10.local_ref, f32[64,4,128]{2,1,0:T(4,128)S(1)} %all_to_all.11.received_ref), custom_call_target="tpu_custom_call" | custom-call | tf_op jit(solution)/shard_map/pallas_call | solution.py:317
